TPU v7x, 512 devices: a whole 4x8x8 slice. The times are simulated.
512 devices in a mesh: head: 8 (over z_hi, core), blk: 64 (over x, z_lo, y).
Axes of the slice: x: 4, y: 8, z: 8 (z_hi: 4, z_lo: 2; z = z_hi * 2 + z_lo), core: 2. Of those that a mesh axis runs over, the one named last changes fastest.
Arguments:
- fresh_query: bfloat16 [3584, 2048], P(('head', 'blk')), may hold values from -5 to 5
- fresh_entries: bfloat16 [2, 3584, 2048], P(None, ('head', 'blk')), may hold values from -5 to 5
- cached_entries: bfloat16 [2, 8192, 2048], P(None, ('head', 'blk')), may hold values from -5 to 5
- recompute_rows: int32 [512, 7], P(('head', 'blk')), may hold values from 0 to 15, as said below
- valid_counts: int32 [512], P(('head', 'blk')), may hold values from 1 to 7, as said below
- out_weight: bfloat16 [2048, 3072], P('head'), may hold values from -0.125 to 0.125
- out_gate: float32 [3072], replicated, may hold values from 0.5 to 2
Outputs:
- updated: bfloat16 [3584, 3072], P(('head', 'blk'))
Inputs may be any that keep to these rules, and one draw needn't show every extreme that they name: `recompute_rows`: within one device the 7 entries name distinct local rows; entries from valid_counts onward are not used. `valid_counts`: some device uses all 7 slots and some only one.
All inputs are finite; a program needn't handle non-finite values.
Results may differ from a plain program's by a relative error of at most 0.018.
Values may be sent and summed in bfloat16 or wider, within the bound.
A program may use at most 64 MiB of HBM per device.

v0:
```python
import jax
import jax.numpy as jnp
from jax import lax
from jax.sharding import PartitionSpec as P

HD = 128


def on_device(
    fresh_query, fresh_entries, cached_entries, recompute_rows, valid_counts, out_weight, out_gate
):
    score_scale = HD ** (-0.5)
    token_count = cached_entries.shape[1]
    slot_count = fresh_query.shape[0]
    slot_index = jnp.arange(slot_count, dtype=jnp.int32)
    valid_slots = slot_index < valid_counts[0]
    picked = (
        recompute_rows[0][None, :] == jnp.arange(token_count, dtype=jnp.int32)[:, None]
    ) & valid_slots[None, :]
    chosen = jnp.einsum(
        "tc,scw->stw",
        picked.astype(jnp.bfloat16),
        fresh_entries,
        preferred_element_type=jnp.float32,
    ).astype(jnp.bfloat16)
    replaced = jnp.any(picked, axis=1)
    merged = jnp.where(replaced[None, :, None], chosen, cached_entries)
    queries, keys_values = (
        lax.all_to_all(fresh_query[None], "head", split_axis=2, concat_axis=1, tiled=True),
        lax.all_to_all(merged, "head", split_axis=2, concat_axis=1, tiled=True),
    )
    queries = queries[0]
    query_rows = queries.shape[0]
    local_heads = queries.shape[1] // HD
    query_heads = queries.reshape(query_rows, local_heads, HD)
    piece = lax.all_gather(keys_values, "blk", axis=1, tiled=True)
    row_top = jnp.full((query_rows, local_heads), -1e30, jnp.float32)
    key_heads = piece[0].reshape(-1, local_heads, HD)
    value_heads = piece[1].reshape(-1, local_heads, HD)
    scores = (
        jnp.einsum("qhd,khd->qhk", query_heads, key_heads, preferred_element_type=jnp.float32)
        * score_scale
    )
    new_top = jnp.maximum(row_top, jnp.max(scores, axis=2))
    weights_raw = jnp.exp(scores - new_top[:, :, None])
    denominator = jnp.sum(weights_raw, axis=2)
    weighted = jnp.einsum(
        "qhk,khd->qhd",
        weights_raw.astype(jnp.bfloat16),
        value_heads,
        preferred_element_type=jnp.float32,
    )
    row_top, denominator, weighted = (new_top, denominator, weighted)
    attention = weighted / denominator[:, :, None]
    attention = attention.reshape(query_rows, local_heads * HD).astype(jnp.bfloat16)
    summed = lax.psum_scatter(
        jnp.dot(attention, out_weight, preferred_element_type=jnp.float32).astype(jnp.bfloat16),
        "head",
        scatter_dimension=0,
        tiled=True,
    ).astype(jnp.float32)
    return jnp.where(valid_slots[:, None], summed * out_gate[None, :], 0.0).astype(jnp.bfloat16)


def solution(mesh):
    in_specs = (
        P(("head", "blk"), None),
        P(None, ("head", "blk"), None),
        P(None, ("head", "blk"), None),
        P(("head", "blk"), None),
        P(("head", "blk")),
        P("head", None),
        P(),
    )
    out_specs = P(("head", "blk"), None)
    return jax.shard_map(
        on_device, mesh=mesh, in_specs=in_specs, out_specs=out_specs, check_vma=False
    )
```

profile of v0, /device:TPU:1, one launch (start us, length us, event | category | flops | bytes accessed | tf_op | source)
XLA Modules:
  0.0 407.0 jit_solution(17147492162300547389)
XLA Ops:
  7.3 0.7 fusion.27
  8.1 1.3 fusion.5
  9.3 0.7 copy.29
  10.1 1.1 reshape.19
  11.1 20.3 %all_to_all.33 = bf16[8,2,4096]{2,1,0:T(2,128)(2,1)S(1)} all-to-all(bf16[8,2,4096]{2,1,0:T(2,128)(2,1)S(1)} %reshape.19), channel_id=1, replica_groups=mesh['head'=8,'blk'=64] {'head'}, dimensions={0} | all-to-all | bytes 262144 | tf_op jit(solution)/shard_map/all_to_all | solution.py:30
  31.5 0.7 reshape.20
  32.2 1.7 copy.44
  33.9 0.9 copy.34
  35.3 11.5 %reduce = bf16[2048,7]{1,0:T(8,128)(2,1)S(1)} reduce(bf16[2048,1,7]{2,1,0:T(2,128)(2,1)S(1)} %bitcast.56, bf16[]{:T(256)} %broadcast.17), dimensions={1}, to_apply=%bitcast.44.reduce_sub_computation | reduce | bytes 57346
  46.9 0.7 reshape.21
  47.6 11.7 %all_to_all.34 = bf16[8,2,896]{2,1,0:T(2,128)(2,1)S(1)} all-to-all(bf16[8,2,896]{2,1,0:T(2,128)(2,1)S(1)} %reshape.21), channel_id=1, replica_groups=mesh['head'=8,'blk'=64] {'head'}, dimensions={0} | all-to-all | bytes 57344 | tf_op jit(solution)/shard_map/all_to_all | solution.py:29
  59.3 1.1 reshape.22
  60.5 0.6 copy.35
  61.1 246.0 %all-gather.2.cloned.1.call-done = bf16[2,8192,256]{2,1,0:T(8,128)(2,1)} async-done(((bf16[2,128,256]{2,1,0:T(8,128)(2,1)}), bf16[2,8192,256]{2,1,0:T(8,128)(2,1)}) %all-gather.2.cloned.1.call-update) | async-done | bytes 8388624 | tf_op jit(solution)/shard_map/all_gather | solution.py:36
  307.1 5.7 %fusion.31 = (bf16[1,8192,256]{2,1,0:T(8,128)(2,1)}, bf16[1,8192,256]{2,1,0:T(8,128)(2,1)}) fusion(bf16[2,8192,256]{2,1,0:T(8,128)(2,1)} %all-gather.2.cloned.1.call-done), kind=kLoop, calls=%fused_computation.29 | loop fusion | bytes 16777216 | tf_op jit(solution)/shard_map/slice | solution.py:38
  312.9 6.4 %copy.33 = bf16[1,8192,256]{1,2,0:T(8,128)(2,1)} copy(bf16[1,8192,256]{2,1,0:T(8,128)(2,1)} %get-tuple-element.5) | data formatting | bytes 8388608 | tf_op jit(solution)/shard_map/slice | solution.py:38
  319.2 4.8 %fusion.32 = (f32[56,2]{0,1:T(2,128)S(1)}, f32[56,2,8192]{2,0,1:T(8,128)}) fusion(bf16[8192,2,128]{0,2,1:T(8,128)(2,1)} %bitcast.53, bf16[56,2,128]{2,1,0:T(2,128)(2,1)S(1)} %reshape_squeeze.11), kind=kOutput, calls=%fused_computation.30 | convolution fusion | flops 236715920 | bytes 7893440 | tf_op jit(solution)/shard_map/qhd,khd->qhk/dot_general | solution.py:41
  324.0 6.4 %copy.32 = bf16[1,8192,256]{1,2,0:T(8,128)(2,1)} copy(bf16[1,8192,256]{2,1,0:T(8,128)(2,1)} %get-tuple-element.6) | data formatting | bytes 8388608 | tf_op jit(solution)/shard_map/slice | solution.py:39
  330.4 2.8 fusion.2
  333.5 3.9 fusion.18
  337.8 54.8 %fusion = bf16[8,3072]{1,0:T(8,128)(2,1)S(1)} fusion(bf16[56,3072]{1,0:T(8,128)(2,1)S(1)} %convolution_convert_fusion), kind=kCustom, calls=%all-reduce-scatter | all-reduce-scatter fusion | flops 196609 | bytes 395264
  392.7 4.3 %collective-permute-start = (bf16[7,3072]{1,0:T(8,128)(2,1)S(1)}, bf16[7,3072]{1,0:T(8,128)(2,1)S(1)}, u32[]{:S(2)}, u32[]{:S(2)}) collective-permute-start(bf16[7,3072]{1,0:T(8,128)(2,1)S(1)} %slice.10), channel_id=1, source_target_pairs={{0,64},{64,128},{128,192},{192,256},{256,320},{320,384},{384,448},... | collective-permute-start | bytes 129032
  396.9 1.3 dynamic-slice.4
  399.5 0.7 select_convert_fusion
  (20 shorter events, 1.9 us)
Async XLA Ops:
  6.5 330.9 %copy-start = (bf16[256,3072]{1,0:T(8,128)(2,1)S(1)}, bf16[256,3072]{1,0:T(8,128)(2,1)}, u32[]{:S(2)}) copy-start(bf16[256,3072]{1,0:T(8,128)(2,1)} %param.12) | copy-start | bytes 4718596
  6.5 27.4 %copy-start.2 = (bf16[7,2048]{1,0:T(8,128)(2,1)S(1)}, bf16[7,2048]{1,0:T(8,128)(2,1)}, u32[]{:S(2)}) copy-start(bf16[7,2048]{1,0:T(8,128)(2,1)} %param.7) | copy-start | bytes 86020
  6.5 300.6 %all-gather.2.cloned.1.call-start = ((), (), s32[]{:S(2)}) async-start(), calls=%async_computation.2 | async-start | bytes 8519680 | tf_op jit(solution)/shard_map/all_gather | solution.py:36
  330.4 3.1 copy-start.1
  333.5 65.9 %copy-start.3 = (f32[3072]{0:T(1024)S(1)}, f32[3072]{0:T(1024)}, u32[]{:S(2)}) copy-start(f32[3072]{0:T(1024)} %param.13) | copy-start | bytes 36868
  392.7 6.6 %collective-permute-start = (bf16[7,3072]{1,0:T(8,128)(2,1)S(1)}, bf16[7,3072]{1,0:T(8,128)(2,1)S(1)}, u32[]{:S(2)}, u32[]{:S(2)}) collective-permute-start(bf16[7,3072]{1,0:T(8,128)(2,1)S(1)} %slice.10), channel_id=1, source_target_pairs={{0,64},{64,128},{128,192},{192,256},{256,320},{320,384},{384,448},... | collective-permute-start | bytes 129032
Sparse Core Ops, SparseCore 0:
  34.0 273.0 all-gather.1
where the time goes:
time: 408 us; the launch traced here: 407 us
  waiting for transfers between devices  246 us (60%)
  blocking collectives  86.9 us (21%)
  local copies, waits for them, and re-layouts  28.3 us (7%)
  other arithmetic  15.8 us (4%)
  between operations  15 us (4%)
  matrix products  10.3 us (3%)
  starting transfers between devices  4.27 us (1%)
    all_gather x1, waiting for transfers between devices, on_device(): piece = lax.all_gather(keys_values, 'blk', axis=1, tiled=True)  246 us
    unnamed x1, blocking collectives  54.8 us
    all_to_all x1, blocking collectives, on_device(): lax.all_to_all(merged, 'head', split_axis=2, concat_axis=1, tiled=True)  20.3 us
    slice x2, local copies, waits for them, and re-layouts, on_device(): key_heads = piece[0].reshape(-1, local_heads, HD)  12.1 us
    all_to_all x1, blocking collectives, on_device(): lax.all_to_all(fresh_query[None], 'head', split_axis=2, concat_axis=1, ti...  11.7 us
    unnamed x1, other arithmetic  11.5 us
  transfers between devices with their start and end apart: 2, of which 2 were waited for; matrix products, arithmetic and copies ran while one was open for 4% of the time, Pallas kernels for 0%

commit v1 on v0

v1 whole, which is shorter than its diff:
```python
import functools
import math

import jax
import jax.numpy as jnp
from jax import lax
from jax.experimental import pallas as pl
from jax.experimental.pallas import tpu as pltpu
from jax.sharding import PartitionSpec as P

HD = 128
HEADS = 16
TOK = 16
CAP = 7
D = 3072
NX, NY, NZ = 4, 8, 4
CHUNKS = 3
HALF = D // 2
CW = HALF // CHUNKS
SCALE2 = (HD ** -0.5) * math.log2(math.e)
MESH = pl.DeviceIdType.MESH
F32, BF16 = jnp.float32, jnp.bfloat16


def kernel(
    q_hbm, fresh_hbm, cached_hbm, rows_ref, cnt_ref, w_hbm, out_ref,
    q_in, fresh_in, cached_in, fresh32, q_out, kv_out, q_land, kv_all, q_all, vt,
    o_out, o_in, st_out, st_in, att, a_in, w_all, p_out, p_in,
    sem_in, qz_s, qz_r, kz_s, kz_r, w_s, w_r, qy_s, qy_r, kx_s, kx_r,
    o_s, o_r, t_s, t_r, a_s, a_r, p_s, p_r,
):
    head = lax.axis_index("head")
    blk = lax.axis_index("blk")
    core = head % 2
    zh = head // 2
    y = blk % NY
    zl = (blk // NY) % 2
    x = blk // (2 * NY)
    me = head * 2 + zl

    def at_z(h):
        return (h // 2, (x * 2 + h % 2) * NY + y)

    def at_x(xx):
        return (head, (xx * 2 + zl) * NY + y)

    def at_y(yy):
        return (head, (x * 2 + zl) * NY + yy)

    def send(src, dst, s_sem, r_sem, dev):
        return pltpu.make_async_remote_copy(
            src_ref=src, dst_ref=dst, send_sem=s_sem, recv_sem=r_sem,
            device_id=dev, device_id_type=MESH,
        )

    right, left = at_x((x + 1) % NX), at_x((x + NX - 1) % NX)

    loads = [
        pltpu.make_async_copy(q_hbm, q_in, sem_in.at[0]),
        pltpu.make_async_copy(fresh_hbm, fresh_in, sem_in.at[1]),
        pltpu.make_async_copy(cached_hbm, cached_in, sem_in.at[2]),
        pltpu.make_async_copy(w_hbm, w_all.at[core], sem_in.at[3]),
    ]
    for load in loads:
        load.start()

    barrier = pltpu.get_barrier_semaphore()

    def greet(t, _):
        pl.semaphore_signal(barrier, inc=1, device_id=at_z((me + t) % HEADS), device_id_type=MESH)
        return 0

    lax.fori_loop(1, HEADS, greet, 0)
    for s in range(1, NY):
        pl.semaphore_signal(barrier, inc=1, device_id=at_y((y + s) % NY), device_id_type=MESH)
    for dev in (right, left):
        pl.semaphore_signal(barrier, inc=1, device_id=dev, device_id_type=MESH)

    loads[0].wait()
    fresh32[0, ...] = jnp.zeros((8, HEADS * HD), F32)
    fresh32[0, 0:CAP, :] = q_in[...].astype(F32)
    for h in range(HEADS):
        rows8 = fresh32[0, :, h * HD:(h + 1) * HD]
        q_out[h] = jnp.concatenate([rows8, jnp.zeros((8, HD), F32)], axis=0).astype(BF16)
    loads[1].wait()
    loads[2].wait()
    for i in range(2):
        fresh32[1 + i, 0:CAP, :] = fresh_in[i].astype(F32)
    count = cnt_ref[0]
    token = lax.broadcasted_iota(jnp.int32, (TOK, HD), 0)
    hits = []
    for c in range(CAP):
        used = jnp.full((TOK, HD), c, jnp.int32) < count
        hits.append((token == rows_ref[0, c]) & used)
    for h in range(HEADS):
        for i in range(2):
            cols = slice(h * HD, (h + 1) * HD)
            merged = cached_in[i, :, cols].astype(F32)
            for c in range(CAP):
                merged = jnp.where(hits[c], fresh32[1 + i, c:c + 1, cols], merged)
            kv_out[h, i * TOK:(i + 1) * TOK, :] = merged.astype(BF16)

    pl.semaphore_wait(barrier, HEADS - 1 + NY - 1 + 2)

    place = (me % 4) * 4 + me // 4
    q_land[place] = q_out[me]
    kv_all[0, 0] = kv_out[me]

    def send_q(t, _):
        h = (me + t) % HEADS
        send(q_out.at[h], q_land.at[place], qz_s.at[t], qz_r.at[t], at_z(h)).start()
        return 0

    def send_kv(t, _):
        h = (me + t) % HEADS
        send(kv_out.at[h], kv_all.at[0, t], kz_s.at[t], kz_r.at[t], at_z(h)).start()
        return 0

    lax.fori_loop(1, HEADS, send_q, 0)
    lax.fori_loop(1, HEADS, send_kv, 0)

    other = (head + 1 - 2 * core, blk)
    w_copy = send(w_hbm, w_all.at[core], w_s, w_r, other)
    w_copy.start()

    def wait_q(t, _):
        h = (me + HEADS - t) % HEADS
        src = (h % 4) * 4 + h // 4
        send(q_out.at[0], q_land.at[src], qz_s.at[t], qz_r.at[t], at_z(h)).wait_recv()
        return 0

    lax.fori_loop(1, HEADS, wait_q, 0)
    q_all[0] = q_land[...].astype(F32)[:, 0:8, :].reshape(HEADS * 8, HD).astype(BF16)
    order = (4, 3, 5, 2, 6, 1, 7)
    for s in order:
        send(q_all.at[0], q_all.at[s], qy_s.at[s], qy_r.at[s], at_y((y + s) % NY)).start()

    lower, upper = pl.ds(0, 8), pl.ds(8, 8)

    def wait_kv(t, _):
        send(kv_out.at[0], kv_all.at[0, t], kz_s.at[t], kz_r.at[t], left).wait_recv()
        return 0

    def kx(i, src, dst, dev):
        return send(kv_all.at[src[0], src[1]], kv_all.at[dst, src[1]], kx_s.at[i], kx_r.at[i], dev)

    copies = [
        kx(0, (0, lower), 1, right),
        kx(1, (0, upper), 2, left),
        kx(2, (0, upper), 1, right),
        kx(3, (0, lower), 2, left),
        kx(4, (1, lower), 3, right),
        kx(5, (2, upper), 3, left),
    ]
    lax.fori_loop(1, 8, wait_kv, 0)
    copies[0].start()
    copies[3].start()
    lax.fori_loop(8, HEADS, wait_kv, 0)
    copies[1].start()
    copies[2].start()
    copies[0].wait_recv()
    copies[4].start()
    copies[1].wait_recv()
    copies[5].start()
    for i in (2, 3, 4, 5):
        copies[i].wait_recv()

    tokens = NX * HEADS * TOK
    keys = kv_all[:, :, 0:TOK, :].reshape(tokens, HD)
    values = kv_all[:, :, TOK:2 * TOK, :].reshape(tokens, HD)
    vt[0:HD, :] = values.astype(F32).T.astype(BF16)
    vt[HD:HD + 16, :] = jnp.ones((16, tokens), BF16)
    for pair in ((4, 3), (5, 2), (6, 1), (7, 0)):
        for s in pair:
            if s:
                send(q_all.at[0], q_all.at[s], qy_s.at[s], qy_r.at[s], left).wait_recv()
        queries = jnp.concatenate([q_all[pair[0]], q_all[pair[1]]], axis=0)
        scores = lax.dot_general(keys, queries, (((1,), (1,)), ((), ())), preferred_element_type=F32)
        top = jnp.max(scores, axis=0, keepdims=True) * SCALE2
        weights = jnp.exp2(scores * SCALE2 - top).astype(BF16)
        mixed = jnp.dot(vt[...], weights, preferred_element_type=F32)
        total = mixed[HD:HD + 1, :]
        mixed = (mixed[0:HD, :] * (1.0 / total)).astype(BF16)
        level = top + jnp.log2(total)
        for n, s in enumerate(pair):
            cols = slice(n * HD, (n + 1) * HD)
            if s == 0:
                o_in[0] = mixed[:, cols]
                st_in[0] = level[:, cols]
            else:
                dev = at_y((y + NY - s) % NY)
                o_out[s] = mixed[:, cols]
                st_out[s] = level[:, cols]
                send(st_out.at[s], st_in.at[s], t_s.at[s], t_r.at[s], dev).start()
                send(o_out.at[s], o_in.at[s], o_s.at[s], o_r.at[s], dev).start()

    for s in range(1, NY):
        send(st_out.at[s], st_in.at[s], t_s.at[s], t_r.at[s], left).wait_recv()
        send(o_out.at[s], o_in.at[s], o_s.at[s], o_r.at[s], left).wait_recv()
    peak = st_in[0]
    for s in range(1, NY):
        peak = jnp.maximum(peak, st_in[s])
    parts = [jnp.exp2(st_in[s] - peak) for s in range(NY)]
    share = 1.0 / functools.reduce(jnp.add, parts)
    mean = functools.reduce(jnp.add, [o_in[s].astype(F32) * (parts[s] * share) for s in range(NY)])
    att[...] = mean.T.astype(BF16)

    def rows_of(quarter):
        return pl.ds(pl.multiple_of(quarter * 32, 32), 32)

    mine = me % 4
    for t in range(1, 4):
        k = (mine + t) % 4
        send(att.at[rows_of(k)], a_in.at[mine], a_s.at[t], a_r.at[t], at_z(zh * 4 + k)).start()
    a_in[mine] = att[rows_of(mine), :]
    loads[3].wait()
    w_wait = send(w_hbm, w_all.at[1 - core], w_s, w_r, other)
    w_wait.wait_recv()
    for t in range(1, 4):
        k = (mine + 4 - t) % 4
        send(att.at[rows_of(0)], a_in.at[k], a_s.at[t], a_r.at[t], left).wait_recv()

    rows = jnp.concatenate([a_in[k] for k in range(4)], axis=1)
    for ci in range(CHUNKS):
        lo, hi = ci * CW, HALF + ci * CW
        sides = []
        for start in (lo, hi):
            w = jnp.concatenate([w_all[0, :, start:start + CW], w_all[1, :, start:start + CW]], axis=0)
            sides.append(jnp.dot(rows, w, preferred_element_type=F32))
        for k in range(NZ):
            block = jnp.concatenate([side[k * 8:(k + 1) * 8] for side in sides], axis=0)
            p_out[ci, k] = block.astype(BF16)
        for t in range(1, NZ):
            k = (zh + t) % NZ
            send(
                p_out.at[ci, k], p_in.at[ci, t], p_s.at[ci, t], p_r.at[ci, t], at_z(k * 4 + mine)
            ).start()
    for ci in range(CHUNKS):
        total = p_out[ci, zh].astype(F32)
        for t in range(1, NZ):
            send(p_out.at[ci, 0], p_in.at[ci, t], p_s.at[ci, t], p_r.at[ci, t], left).wait_recv()
            total = total + p_in[ci, t].astype(F32)
        out_ref[:, ci * CW:(ci + 1) * CW] = total[0:8]
        out_ref[:, HALF + ci * CW:HALF + (ci + 1) * CW] = total[8:16]

    def sent_z(t, _):
        send(q_out.at[0], q_land.at[0], qz_s.at[t], qz_r.at[t], left).wait_send()
        send(kv_out.at[0], kv_all.at[0, 0], kz_s.at[t], kz_r.at[t], left).wait_send()
        return 0

    lax.fori_loop(1, HEADS, sent_z, 0)
    w_copy.wait_send()
    for s in range(1, NY):
        send(q_all.at[0], q_all.at[s], qy_s.at[s], qy_r.at[s], left).wait_send()
        send(st_out.at[s], st_in.at[s], t_s.at[s], t_r.at[s], left).wait_send()
        send(o_out.at[s], o_in.at[s], o_s.at[s], o_r.at[s], left).wait_send()
    for copy in copies:
        copy.wait_send()
    for t in range(1, 4):
        send(att.at[rows_of(0)], a_in.at[0], a_s.at[t], a_r.at[t], left).wait_send()
        for ci in range(CHUNKS):
            send(p_out.at[ci, 0], p_in.at[ci, t], p_s.at[ci, t], p_r.at[ci, t], left).wait_send()


def on_device(fresh_query, fresh_entries, cached_entries, recompute_rows, valid_counts, out_weight, out_gate):
    dma = pltpu.SemaphoreType.DMA
    any_space = pl.BlockSpec(memory_space=pl.ANY)
    smem = pl.BlockSpec(memory_space=pltpu.SMEM)
    width = HEADS * HD
    summed = pl.pallas_call(
        kernel,
        out_shape=jax.ShapeDtypeStruct((8, D), F32),
        in_specs=[any_space, any_space, any_space, smem, smem, any_space],
        out_specs=pl.BlockSpec(memory_space=pltpu.VMEM),
        scratch_shapes=[
            pltpu.VMEM((CAP, width), BF16),
            pltpu.VMEM((2, CAP, width), BF16),
            pltpu.VMEM((2, TOK, width), BF16),
            pltpu.VMEM((3, 8, width), F32),
            pltpu.VMEM((HEADS, 16, HD), BF16),
            pltpu.VMEM((HEADS, 2 * TOK, HD), BF16),
            pltpu.VMEM((HEADS, 16, HD), BF16),
            pltpu.VMEM((NX, HEADS, 2 * TOK, HD), BF16),
            pltpu.VMEM((NY, HEADS * 8, HD), BF16),
            pltpu.VMEM((HD + 16, NX * HEADS * TOK), BF16),
            pltpu.VMEM((NY, HD, HD), BF16),
            pltpu.VMEM((NY, HD, HD), BF16),
            pltpu.VMEM((NY, 1, HD), F32),
            pltpu.VMEM((NY, 1, HD), F32),
            pltpu.VMEM((HD, HD), BF16),
            pltpu.VMEM((4, 32, HD), BF16),
            pltpu.VMEM((2, 2 * HD, D), BF16),
            pltpu.VMEM((CHUNKS, NZ, 16, CW), BF16),
            pltpu.VMEM((CHUNKS, NZ, 16, CW), BF16),
            dma((4,)),
            dma((HEADS,)), dma((HEADS,)), dma((HEADS,)), dma((HEADS,)),
            dma, dma,
            dma((NY,)), dma((NY,)),
            dma((6,)), dma((6,)),
            dma((NY,)), dma((NY,)), dma((NY,)), dma((NY,)),
            dma((4,)), dma((4,)),
            dma((CHUNKS, NZ)), dma((CHUNKS, NZ)),
        ],
        compiler_params=pltpu.CompilerParams(
            collective_id=0, has_side_effects=True, vmem_limit_bytes=48 * 1024 * 1024
        ),
    )(fresh_query, fresh_entries, cached_entries, recompute_rows, valid_counts, out_weight)
    valid = jnp.arange(CAP, dtype=jnp.int32) < valid_counts[0]
    return jnp.where(valid[:, None], summed[:CAP] * out_gate[None, :], 0.0).astype(BF16)


def solution(mesh):
    both = ("head", "blk")
    in_specs = (P(both, None), P(None, both, None), P(None, both, None), P(both, None), P(both), P("head", None), P())
    return jax.shard_map(on_device, mesh=mesh, in_specs=in_specs, out_specs=P(both, None), check_vma=False)
```

time: 408 us -> 57.1 us (0.14)
  waiting for transfers between devices: 246 us -> 0 us
  blocking collectives: 86.9 us -> 0 us
  Pallas kernels: 0 us -> 50.8 us
  local copies, waits for them, and re-layouts: 28.3 us -> 4.57 us
  other arithmetic: 15.8 us -> 0.7 us
  between operations: 15 us -> 0.7 us
  matrix products: 10.3 us -> 0 us
  starting transfers between devices: 4.27 us -> 0 us
    all_gather x1 -> x0, waiting for transfers between devices: 246 us -> none  [on_device(): piece = lax.all_gather(keys_values, 'blk', axis=1, tiled=True)]
    unnamed x1 -> x0, blocking collectives: 54.8 us -> none
    pallas_call x0 -> x1, Pallas kernels: none -> 50.8 us  [on_device(): pl.pallas_call(kernel, out_shape=jax.ShapeDtypeStruct((8, D), F32), in_sp...]
    all_to_all x2 -> x0, blocking collectives: 32.1 us -> none  [the longest x1 20.3 us: on_device(): lax.all_to_all(merged, 'head', split_axis=2, concat_axis=1, tiled=True)]
    slice x3 -> x0, local copies, waits for them, and re-layouts: 18.5 us -> none  [the longest x2 12.1 us: on_device(): key_heads = piece[0].reshape(-1, local_heads, HD)]
    unnamed x1 -> x0, other arithmetic: 11.5 us -> none
    dot_general x4 -> x0, matrix products: 10.3 us -> none  [the longest x1 4.78 us: on_device(): jnp.einsum('qhd,khd->qhk', query_heads, key_heads, preferred_element_type...]
    unnamed x1 -> x0, starting transfers between devices: 4.27 us -> none
  transfers between devices with their start and end apart: 2 -> 0, of which waited for: 2 -> 0; matrix products, arithmetic and copies ran while one was open for 4% -> 0% of each run, Pallas kernels for 0% -> 0%
where the time goes in v1:
time: 57.1 us; the launch traced here: 56.8 us
  Pallas kernels  50.8 us (89%)
  local copies, waits for them, and re-layouts  4.57 us (8%)
  other arithmetic  0.7 us (1%)
  between operations  0.7 us (1%)
    pallas_call x1, Pallas kernels, on_device(): pl.pallas_call(kernel, out_shape=jax.ShapeDtypeStruct((8, D), F32), in_sp...  50.8 us
    unnamed x11, local copies, waits for them, and re-layouts  4.57 us

profile of v1, /device:TPU:1, one launch (start us, length us, event | category | flops | bytes accessed | tf_op | source)
XLA Modules:
  0.0 56.8 jit_solution(14930138607987635109)
XLA Ops:
  0.0 0.0 copy-start.4
  0.7 0.8 %copy.8.fresh_hbm = bf16[2,7,2048]{2,1,0:T(8,128)(2,1)S(1)} copy(bf16[2,7,2048]{2,0,1:T(2,128)(2,1)} %param.8) | data formatting | bytes 114688 | tf_op args[1]
  1.5 0.0 copy-start
  1.5 1.4 %copy-done = bf16[256,3072]{1,0:T(8,128)(2,1)S(1)} copy-done((bf16[256,3072]{1,0:T(8,128)(2,1)S(1)}, bf16[256,3072]{1,0:T(8,128)(2,1)}, u32[]{:S(2)}) %copy-start) | copy-done | bytes 1572888
  2.9 0.0 copy-start.1
  2.9 0.9 %copy-done.1 = bf16[2,16,2048]{2,1,0:T(8,128)(2,1)S(1)} copy-done((bf16[2,16,2048]{2,1,0:T(8,128)(2,1)S(1)}, bf16[2,16,2048]{2,1,0:T(8,128)(2,1)}, u32[]{:S(2)}) %copy-start.1) | copy-done | bytes 131096
  3.8 0.0 copy-start.2
  3.8 0.8 %copy-done.2 = bf16[7,2048]{1,0:T(8,128)(2,1)S(1)} copy-done((bf16[7,2048]{1,0:T(8,128)(2,1)S(1)}, bf16[7,2048]{1,0:T(8,128)(2,1)}, u32[]{:S(2)}) %copy-start.2) | copy-done | bytes 28696
  4.6 0.0 copy-start.3
  4.6 0.7 %copy-done.3 = s32[1,7]{1,0:T(1,128)S(1)} copy-done((s32[1,7]{1,0:T(1,128)S(1)}, s32[1,7]{1,0:T(1,128)}, u32[]{:S(2)}) %copy-start.3) | copy-done | bytes 52
  5.2 50.8 %shard_map.73 = f32[8,3072]{1,0:T(8,128)S(1)} custom-call(bf16[7,2048]{1,0:T(8,128)(2,1)S(1)} %copy-done.2, bf16[2,7,2048]{2,1,0:T(8,128)(2,1)S(1)} %copy.8.fresh_hbm, bf16[2,16,2048]{2,1,0:T(8,128)(2,1)S(1)} %copy-done.1, s32[1,7]{1,0:T(1,128)S(1)} %copy-done.3, s32[1]{0:T(128)} %copy.9.cnt_ref, bf16[256,3072]{1,0:T(8,128)(2,1)S(1)} %copy-done), custom_call_target="tpu_custom_call" | custom-call | tf_op jit(solution)/shard_map/pallas_call | solution.py:270
  56.1 0.0 copy-done.4
  56.1 0.7 %select_convert_fusion = bf16[7,3072]{1,0:T(8,128)(2,1)} fusion(f32[8,3072]{1,0:T(8,128)S(1)} %shard_map.73, f32[3072]{0:T(1024)S(1)} %copy-done.4, pred[7]{0:T(512)(128)(4,1)S(1)} %iota_compare_fusion), kind=kLoop, calls=%fused_computation | loop fusion | flops 64512 | bytes 141319 | tf_op jit(solution)/shard_map/convert_element_type | solution.py:309
  (1 shorter events, 0.0 us)
Async XLA Ops:
  0.0 56.1 %copy-start.4 = (f32[3072]{0:T(1024)S(1)}, f32[3072]{0:T(1024)}, u32[]{:S(2)}) copy-start(f32[3072]{0:T(1024)} %param.13) | copy-start | bytes 36868
  1.5 1.4 %copy-start = (bf16[256,3072]{1,0:T(8,128)(2,1)S(1)}, bf16[256,3072]{1,0:T(8,128)(2,1)}, u32[]{:S(2)}) copy-start(bf16[256,3072]{1,0:T(8,128)(2,1)} %w_hbm.1) | copy-start | bytes 4718596
  2.9 0.9 %copy-start.1 = (bf16[2,16,2048]{2,1,0:T(8,128)(2,1)S(1)}, bf16[2,16,2048]{2,1,0:T(8,128)(2,1)}, u32[]{:S(2)}) copy-start(bf16[2,16,2048]{2,1,0:T(8,128)(2,1)} %cached_hbm.1) | copy-start | bytes 393220
  3.8 0.8 %copy-start.2 = (bf16[7,2048]{1,0:T(8,128)(2,1)S(1)}, bf16[7,2048]{1,0:T(8,128)(2,1)}, u32[]{:S(2)}) copy-start(bf16[7,2048]{1,0:T(8,128)(2,1)} %q_hbm.1) | copy-start | bytes 86020
  4.6 0.7 %copy-start.3 = (s32[1,7]{1,0:T(1,128)S(1)}, s32[1,7]{1,0:T(1,128)}, u32[]{:S(2)}) copy-start(s32[1,7]{1,0:T(1,128)} %rows_ref.1) | copy-start | bytes 88

commit v2 on v1

--- a/solution.py
+++ b/solution.py
@@ -23,8 +23,8 @@
 
 
 def kernel(
-    q_hbm, fresh_hbm, cached_hbm, rows_ref, cnt_ref, w_hbm, out_ref,
-    q_in, fresh_in, cached_in, fresh32, q_out, kv_out, q_land, kv_all, q_all, vt,
+    q_hbm, fresh_hbm, cached_hbm, rows_hbm, cnt_hbm, w_hbm, out_ref,
+    q_in, fresh_in, cached_in, rows_in, cnt_in, fresh32, q_out, kv_out, q_land, kv_all, q_all, vt,
     o_out, o_in, st_out, st_in, att, a_in, w_all, p_out, p_in,
     sem_in, qz_s, qz_r, kz_s, kz_r, w_s, w_r, qy_s, qy_r, kx_s, kx_r,
     o_s, o_r, t_s, t_r, a_s, a_r, p_s, p_r,
@@ -60,6 +60,8 @@
         pltpu.make_async_copy(fresh_hbm, fresh_in, sem_in.at[1]),
         pltpu.make_async_copy(cached_hbm, cached_in, sem_in.at[2]),
         pltpu.make_async_copy(w_hbm, w_all.at[core], sem_in.at[3]),
+        pltpu.make_async_copy(rows_hbm, rows_in, sem_in.at[4]),
+        pltpu.make_async_copy(cnt_hbm, cnt_in, sem_in.at[5]),
     ]
     for load in loads:
         load.start()
@@ -82,16 +84,16 @@
     for h in range(HEADS):
         rows8 = fresh32[0, :, h * HD:(h + 1) * HD]
         q_out[h] = jnp.concatenate([rows8, jnp.zeros((8, HD), F32)], axis=0).astype(BF16)
-    loads[1].wait()
-    loads[2].wait()
+    for i in (1, 2, 4, 5):
+        loads[i].wait()
     for i in range(2):
-        fresh32[1 + i, 0:CAP, :] = fresh_in[i].astype(F32)
-    count = cnt_ref[0]
+        fresh32[1 + i, 0:CAP, :] = fresh_in[:, i, :].astype(F32)
+    count = cnt_in[0]
     token = lax.broadcasted_iota(jnp.int32, (TOK, HD), 0)
     hits = []
     for c in range(CAP):
         used = jnp.full((TOK, HD), c, jnp.int32) < count
-        hits.append((token == rows_ref[0, c]) & used)
+        hits.append((token == rows_in[0, c]) & used)
     for h in range(HEADS):
         for i in range(2):
             cols = slice(h * HD, (h + 1) * HD)
@@ -265,17 +267,18 @@
 def on_device(fresh_query, fresh_entries, cached_entries, recompute_rows, valid_counts, out_weight, out_gate):
     dma = pltpu.SemaphoreType.DMA
     any_space = pl.BlockSpec(memory_space=pl.ANY)
-    smem = pl.BlockSpec(memory_space=pltpu.SMEM)
     width = HEADS * HD
     summed = pl.pallas_call(
         kernel,
         out_shape=jax.ShapeDtypeStruct((8, D), F32),
-        in_specs=[any_space, any_space, any_space, smem, smem, any_space],
+        in_specs=[any_space] * 6,
         out_specs=pl.BlockSpec(memory_space=pltpu.VMEM),
         scratch_shapes=[
             pltpu.VMEM((CAP, width), BF16),
-            pltpu.VMEM((2, CAP, width), BF16),
+            pltpu.VMEM((CAP, 2, width), BF16),
             pltpu.VMEM((2, TOK, width), BF16),
+            pltpu.SMEM((1, CAP), jnp.int32),
+            pltpu.SMEM((1,), jnp.int32),
             pltpu.VMEM((3, 8, width), F32),
             pltpu.VMEM((HEADS, 16, HD), BF16),
             pltpu.VMEM((HEADS, 2 * TOK, HD), BF16),
@@ -292,7 +295,7 @@
             pltpu.VMEM((2, 2 * HD, D), BF16),
             pltpu.VMEM((CHUNKS, NZ, 16, CW), BF16),
             pltpu.VMEM((CHUNKS, NZ, 16, CW), BF16),
-            dma((4,)),
+            dma((6,)),
             dma((HEADS,)), dma((HEADS,)), dma((HEADS,)), dma((HEADS,)),
             dma, dma,
             dma((NY,)), dma((NY,)),
@@ -302,9 +305,9 @@
             dma((CHUNKS, NZ)), dma((CHUNKS, NZ)),
         ],
         compiler_params=pltpu.CompilerParams(
-            collective_id=0, has_side_effects=True, vmem_limit_bytes=48 * 1024 * 1024
+            collective_id=0, has_side_effects=True, vmem_limit_bytes=60 * 1024 * 1024
         ),
-    )(fresh_query, fresh_entries, cached_entries, recompute_rows, valid_counts, out_weight)
+    )(fresh_query, fresh_entries.transpose(1, 0, 2), cached_entries, recompute_rows, valid_counts, out_weight)
     valid = jnp.arange(CAP, dtype=jnp.int32) < valid_counts[0]
     return jnp.where(valid[:, None], summed[:CAP] * out_gate[None, :], 0.0).astype(BF16)
 

time: 57.1 us -> 53 us (0.928)
  local copies, waits for them, and re-layouts: 4.57 us -> 0.01 us
  other arithmetic: 0.7 us -> 1.59 us
    unnamed x11 -> x2, local copies, waits for them, and re-layouts: 4.57 us -> 0.01 us
    convert_element_type x1, other arithmetic: 0.7 us -> 1.59 us  [on_device(): jnp.where(valid[:, None], summed[:CAP] * out_gate[None, :], 0.0)]
where the time goes in v2:
time: 53 us; the launch traced here: 52.8 us
  Pallas kernels  50.6 us (95%)
  other arithmetic  1.59 us (3%)
  between operations  0.69 us (1%)
    pallas_call x1, Pallas kernels, on_device(): pl.pallas_call(kernel, out_shape=jax.ShapeDtypeStruct((8, D), F32), in_sp...  50.6 us
    convert_element_type x1, other arithmetic, on_device(): jnp.where(valid[:, None], summed[:CAP] * out_gate[None, :], 0.0)  1.59 us

profile of v2, /device:TPU:1, one launch (start us, length us, event | category | flops | bytes accessed | tf_op | source)
XLA Modules:
  0.0 52.8 jit_solution(4767396229770935437)
XLA Ops:
  0.0 0.0 copy-start
  0.7 50.6 %shard_map.73 = f32[8,3072]{1,0:T(8,128)} custom-call(bf16[7,2048]{1,0:T(8,128)(2,1)} %q_hbm.1, bf16[7,2,2048]{2,1,0:T(2,128)(2,1)} %bitcast.3, bf16[2,16,2048]{2,1,0:T(8,128)(2,1)} %cached_hbm.1, s32[1,7]{1,0:T(1,128)} %rows_hbm.1, s32[1]{0:T(128)} %copy.8.cnt_hbm, bf16[256,3072]{1,0:T(8,128)(2,1)} %w_hbm.1), custom_call_target="tpu_custom_call" | custom-call | tf_op jit(solution)/shard_map/pallas_call | solution.py:271
  51.2 0.0 copy-done
  51.3 1.6 %select_convert_fusion = bf16[7,3072]{1,0:T(8,128)(2,1)} fusion(f32[8,3072]{1,0:T(8,128)} %shard_map.73, f32[3072]{0:T(1024)S(1)} %copy-done, pred[7]{0:T(512)(128)(4,1)S(1)} %iota_compare_fusion), kind=kLoop, calls=%fused_computation | loop fusion | flops 64512 | bytes 141319 | tf_op jit(solution)/shard_map/convert_element_type | solution.py:312
  (1 shorter events, 0.0 us)
Async XLA Ops:
  0.0 51.3 %copy-start = (f32[3072]{0:T(1024)S(1)}, f32[3072]{0:T(1024)}, u32[]{:S(2)}) copy-start(f32[3072]{0:T(1024)} %param.13) | copy-start | bytes 36868

commit v3 on v0

v3 whole, which is shorter than its diff:
```python
import functools
import math

import jax
import jax.numpy as jnp
from jax import lax
from jax.experimental import pallas as pl
from jax.experimental.pallas import tpu as pltpu
from jax.sharding import PartitionSpec as P

HD = 128
HEADS = 16
TOK = 16
CAP = 7
D = 3072
NX, NY, NZ, CHIPS = 4, 8, 4, 8
CHUNKS = 3
HALF = D // 2
CW = HALF // CHUNKS
SCALE2 = (HD ** -0.5) * math.log2(math.e)
MESH = pl.DeviceIdType.MESH
F32, BF16 = jnp.float32, jnp.bfloat16

GROUPS = ((1, 7), (2, 6), (3, 5), (0, 4))
SLOT = {(dz, dc): g * 4 + dc * 2 + e for g, pair in enumerate(GROUPS) for e, dz in enumerate(pair) for dc in range(2)}
SELF = SLOT[0, 0]
NEAR_FIRST = sorted((k for k in SLOT if k != (0, 0)), key=lambda k: min(k[0], CHIPS - k[0]))
FAR_FIRST = NEAR_FIRST[::-1]
PAIRS = ((4, 3), (5, 2), (6, 1), (7, 0))


def kernel(
    q_hbm, fresh_hbm, cached_hbm, rows_hbm, cnt_hbm, w_hbm, out_ref,
    q_in, fresh_in, cached_in, rows_in, cnt_in, fresh32, q_out, kv_out, q_land, kv_all, q_all, vt,
    top_ref, mix_ref, o_out, o_in, st_out, st_in, w_all, p_out, p_in,
    sem_in, qz_s, qz_r, kz_s, kz_r, w_s, w_r, qy_s, qy_r, kx_s, kx_r, o_s, o_r, t_s, t_r, p_s, p_r,
):
    head = lax.axis_index("head")
    blk = lax.axis_index("blk")
    core = head % 2
    zh = head // 2
    y = blk % NY
    zl = (blk // NY) % 2
    x = blk // (2 * NY)
    chip = zh * 2 + zl

    def at_z(dz, dc):
        z, c = (chip + dz) % CHIPS, (core + dc) % 2
        return ((z // 2) * 2 + c, (x * 2 + z % 2) * NY + y)

    def head_of(dz, dc):
        z, c = (chip + dz) % CHIPS, (core + dc) % 2
        return (z // 2) * 4 + c * 2 + z % 2

    def at_x(dx):
        return (head, (((x + dx) % NX) * 2 + zl) * NY + y)

    def at_y(dy):
        return (head, (x * 2 + zl) * NY + (y + dy) % NY)

    def at_o(dy, odd, dc):
        return (zh * 2 + (core + dc) % 2, (x * 2 + (zl + odd) % 2) * NY + (y + dy) % NY)

    def at_p(b):
        return (((zh + b) % NZ) * 2 + core, blk)

    def send(src, dst, s_sem, r_sem, dev):
        return pltpu.make_async_remote_copy(
            src_ref=src, dst_ref=dst, send_sem=s_sem, recv_sem=r_sem,
            device_id=dev, device_id_type=MESH,
        )

    loads = [
        pltpu.make_async_copy(q_hbm, q_in, sem_in.at[0]),
        pltpu.make_async_copy(fresh_hbm, fresh_in, sem_in.at[1]),
        pltpu.make_async_copy(cached_hbm, cached_in, sem_in.at[2]),
        pltpu.make_async_copy(rows_hbm, rows_in, sem_in.at[3]),
        pltpu.make_async_copy(cnt_hbm, cnt_in, sem_in.at[4]),
        pltpu.make_async_copy(w_hbm, w_all.at[0], sem_in.at[5]),
    ]
    for load in loads[:5]:
        load.start()

    barrier = pltpu.get_barrier_semaphore()
    partners = [at_z(dz, dc) for dz, dc in FAR_FIRST]
    partners += [at_y(dy) for dy in (4, 3, 5, 2, 6, 1, 7)] + [at_x(dx) for dx in (2, 1, 3)]
    for dev in partners:
        pl.semaphore_signal(barrier, inc=1, device_id=dev, device_id_type=MESH)

    loads[0].wait()
    fresh32[0, ...] = jnp.zeros((8, HEADS * HD), F32)
    fresh32[0, 0:CAP, :] = q_in[...].astype(F32)

    def lanes(h):
        return pl.ds(pl.multiple_of(h * HD, HD), HD)

    for place in [(0, 0)] + FAR_FIRST:
        rows8 = fresh32[0, :, lanes(head_of(*place))]
        q_out[SLOT[place]] = jnp.concatenate([rows8, jnp.zeros((8, HD), F32)], axis=0).astype(BF16)
    q_land[SELF] = q_out[SELF]
    pl.semaphore_wait(barrier, len(partners))

    def z_copy(out, land, s_sem, r_sem, place):
        back = SLOT[(CHIPS - place[0]) % CHIPS, place[1]]
        return send(out.at[SLOT[place]], land.at[back], s_sem.at[SLOT[place]], r_sem.at[back], at_z(*place))

    for place in FAR_FIRST:
        z_copy(q_out, q_land, qz_s, qz_r, place).start()

    for i in (1, 2, 3, 4):
        loads[i].wait()
    for i in range(2):
        fresh32[1 + i, 0:CAP, :] = fresh_in[:, i, :].astype(F32)
    count = cnt_in[0, 0]
    token = lax.broadcasted_iota(jnp.int32, (TOK, HD), 0)
    hits = []
    for c in range(CAP):
        used = jnp.full((TOK, HD), c, jnp.int32) < count
        hits.append((token == rows_in[0, c]) & used)

    def merged(h, i):
        rows = cached_in[i, :, lanes(h)].astype(F32)
        for c in range(CAP):
            rows = jnp.where(hits[c], fresh32[1 + i, c:c + 1, lanes(h)], rows)
        return rows.astype(BF16)

    for place in NEAR_FIRST:
        for i in range(2):
            kv_out[SLOT[place], i * TOK:(i + 1) * TOK, :] = merged(head_of(*place), i)
        z_copy(kv_out, kv_all.at[0], kz_s, kz_r, place).start()
    for i in range(2):
        kv_all[0, SELF, i * TOK:(i + 1) * TOK, :] = merged(head_of(0, 0), i)

    loads[5].start()
    w_copy = send(w_hbm, w_all.at[1], w_s, w_r, at_z(0, 1))
    w_copy.start()

    def qy(g, s):
        part = pl.ds(g * 32, 32)
        return send(q_all.at[0, part], q_all.at[s, part], qy_s.at[g, s], qy_r.at[g, s], at_y(s))

    def kx(g, s):
        part = pl.ds(g * 4, 4)
        return send(kv_all.at[0, part], kv_all.at[s, part], kx_s.at[g, s], kx_r.at[g, s], at_x(s))

    for g in range(4):
        for n in range(g * 4, g * 4 + 4):
            if n != SELF:
                send(q_out.at[n], q_land.at[n], qz_s.at[n], qz_r.at[n], at_x(1)).wait_recv()
        packed = q_land[g * 4:(g + 1) * 4].astype(F32)[:, 0:8, :].reshape(32, HD)
        q_all[0, g * 32:(g + 1) * 32, :] = packed.astype(BF16)
        for s in (4, 3, 5, 2, 6, 1, 7):
            qy(g, s).start()
    for g in range(4):
        for n in range(g * 4, g * 4 + 4):
            if n != SELF:
                send(kv_out.at[n], kv_all.at[0, n], kz_s.at[n], kz_r.at[n], at_x(1)).wait_recv()
        for s in (2, 1, 3):
            kx(g, s).start()

    tokens = HEADS * TOK
    vt[HD:HD + 16, :] = jnp.ones((16, tokens), BF16)

    def attend(slot, number, first):
        keys = kv_all[slot, :, 0:TOK, :].reshape(tokens, HD)
        queries = jnp.concatenate([q_all[s] for s in PAIRS[number]], axis=0)
        scores = lax.dot_general(keys, queries, (((1,), (1,)), ((), ())), preferred_element_type=F32)
        top = jnp.max(scores, axis=0, keepdims=True) * SCALE2
        if not first:
            old = top_ref[number]
            top = jnp.maximum(top, old)
        weights = jnp.exp2(scores * SCALE2 - top).astype(BF16)
        mixed = jnp.dot(vt[...], weights, preferred_element_type=F32)
        if not first:
            mixed = mixed + mix_ref[number] * jnp.exp2(old - top)
        return top, mixed

    def t_copy(s, g):
        dev = at_o(NY - s, 1 - g // 2, g % 2)
        return send(st_out.at[s], st_in.at[g, s], t_s.at[s, g], t_r.at[s, g], dev)

    def o_copy(s, g):
        dev = at_o(NY - s, 1 - g // 2, g % 2)
        return send(o_out.at[s, :, g], o_in.at[g, :, s], o_s.at[s, g], o_r.at[s, g], dev)

    for step, slot in enumerate((0, 1, 3, 2)):
        if slot:
            for g in range(4):
                kx(g, slot).wait_recv()
        vt[0:HD, :] = kv_all[slot, :, TOK:2 * TOK, :].reshape(tokens, HD).astype(F32).T.astype(BF16)
        for number in (3, 2, 1, 0) if step == 0 else (0, 1, 2, 3):
            if step == 0:
                for s in PAIRS[number]:
                    if s:
                        for g in range(4):
                            qy(g, s).wait_recv()
            top, mixed = attend(slot, number, step == 0)
            if step < NX - 1:
                top_ref[number] = top
                mix_ref[number] = mixed
                continue
            total = mixed[HD:HD + 1, :]
            level = top + jnp.log2(total)
            rows = (mixed[0:HD, :] * (1.0 / total)).T.astype(BF16)
            for n, s in enumerate(PAIRS[number]):
                st_out[s] = level[:, n * HD:(n + 1) * HD]
                o_out[s] = rows[n * HD:(n + 1) * HD].reshape(2, 4, 16, HD)
                for g in range(4):
                    if (s, g) != (0, 2):
                        t_copy(s, g).start()
                        o_copy(s, g).start()
    st_in[2, 0] = st_out[0]
    o_in[2, :, 0] = o_out[0, :, 2]

    remote = [(s, g) for s in (4, 3, 5, 2, 6, 1, 7, 0) for g in range(4) if (s, g) != (0, 2)]
    for s, g in remote:
        t_copy(s, g).wait_recv()
    levels = []
    row8 = lax.broadcasted_iota(jnp.int32, (8, HD), 0)
    lane8 = lax.broadcasted_iota(jnp.int32, (8, HD), 1)
    for g in range(4):
        seen = jnp.concatenate([st_in[g, s] for s in range(NY)], axis=0)
        seen = pltpu.roll(seen, 0, 1, stride=16, stride_axis=0)
        for i in range(2):
            moved = pltpu.roll(seen, (HD - i * 64 - g * 16) % HD, 1)
            levels.append(jnp.sum(jnp.where(lane8 // 16 == row8, moved, 0.0), axis=0, keepdims=True))
    levels = jnp.concatenate(levels, axis=0)
    peak = levels
    for shift in (16, 32, 64):
        peak = jnp.maximum(peak, pltpu.roll(peak, shift, 1))
    parts = jnp.exp2(levels - peak)
    total = parts
    for shift in (16, 32, 64):
        total = total + pltpu.roll(total, shift, 1)
    shares = parts / total

    row = lax.broadcasted_iota(jnp.int32, (32, HD), 0)
    lane = lax.broadcasted_iota(jnp.int32, (32, HD), 1)
    owner = row // 8

    def wanted(order):
        block = jnp.where(owner == 0, order[0], jnp.where(owner == 1, order[1], jnp.where(owner == 2, order[2], order[3])))
        return block * 8 + row % 8

    even = wanted((2, 0, 3, 1))
    odd = jnp.where(zl == 1, wanted((0, 2, 3, 1)), wanted((1, 0, 2, 3)))
    for s, g in remote:
        o_copy(s, g).wait_recv()
    mean = []
    for g in range(4):
        place = odd if g < 2 else even
        mix = [
            jnp.where(place == i * 16 + lane % 16, shares[g * 2 + i:g * 2 + i + 1, :], 0.0) for i in range(2)
        ]
        mix = jnp.concatenate(mix, axis=1).astype(BF16)
        mean.append(jnp.dot(mix, o_in[g].reshape(2 * HD, HD), preferred_element_type=F32))
    heads4 = [jnp.where(zl == z, mean[2 + dc], mean[dc]) for dc in range(2) for z in range(2)]
    rows = jnp.concatenate(heads4, axis=1).astype(BF16)

    loads[5].wait()
    send(w_hbm, w_all.at[1], w_s, w_r, at_z(0, 1)).wait_recv()

    def p_copy(ci, b):
        return send(p_out.at[ci, b], p_in.at[ci, b], p_s.at[ci, b], p_r.at[ci, b], at_p(b))

    for ci in range(CHUNKS):
        sides = []
        for start in (ci * CW, HALF + ci * CW):
            w = jnp.concatenate([w_all[0, :, start:start + CW], w_all[1, :, start:start + CW]], axis=0)
            sides.append(jnp.dot(rows, w, preferred_element_type=F32))
        for b in (2, 1, 3, 0):
            block = jnp.concatenate([side[b * 8:(b + 1) * 8] for side in sides], axis=0)
            p_out[ci, b] = block.astype(BF16)
            if b:
                p_copy(ci, b).start()
    valid = lax.broadcasted_iota(jnp.int32, (8, CW), 0) < count
    for ci in range(CHUNKS):
        total = p_out[ci, 0].astype(F32)
        for b in (1, 3, 2):
            p_copy(ci, b).wait_recv()
            total = total + p_in[ci, b].astype(F32)
        out_ref[:, ci * CW:(ci + 1) * CW] = jnp.where(valid, total[0:8], 0.0)
        out_ref[:, HALF + ci * CW:HALF + (ci + 1) * CW] = jnp.where(valid, total[8:16], 0.0)

    for place in NEAR_FIRST:
        z_copy(q_out, q_land, qz_s, qz_r, place).wait_send()
        z_copy(kv_out, kv_all.at[0], kz_s, kz_r, place).wait_send()
    w_copy.wait_send()
    for g in range(4):
        for s in range(1, NY):
            qy(g, s).wait_send()
        for s in range(1, NX):
            kx(g, s).wait_send()
    for s, g in remote:
        t_copy(s, g).wait_send()
        o_copy(s, g).wait_send()
    for ci in range(CHUNKS):
        for b in range(1, NZ):
            p_copy(ci, b).wait_send()


def on_device(fresh_query, fresh_entries, cached_entries, recompute_rows, valid_counts, out_weight, out_gate):
    dma = pltpu.SemaphoreType.DMA
    width = HEADS * HD
    summed = pl.pallas_call(
        kernel,
        out_shape=jax.ShapeDtypeStruct((8, D), F32),
        in_specs=[pl.BlockSpec(memory_space=pl.ANY)] * 6,
        out_specs=pl.BlockSpec(memory_space=pltpu.VMEM),
        scratch_shapes=[
            pltpu.VMEM((CAP, width), BF16),
            pltpu.VMEM((CAP, 2, width), BF16),
            pltpu.VMEM((2, TOK, width), BF16),
            pltpu.SMEM((1, CAP), jnp.int32),
            pltpu.SMEM((1, 1), jnp.int32),
            pltpu.VMEM((3, 8, width), F32),
            pltpu.VMEM((HEADS, 16, HD), BF16),
            pltpu.VMEM((HEADS, 2 * TOK, HD), BF16),
            pltpu.VMEM((HEADS, 16, HD), BF16),
            pltpu.VMEM((NX, HEADS, 2 * TOK, HD), BF16),
            pltpu.VMEM((NY, HEADS * 8, HD), BF16),
            pltpu.VMEM((HD + 16, HEADS * TOK), BF16),
            pltpu.VMEM((4, 1, 2 * HD), F32),
            pltpu.VMEM((4, HD + 16, 2 * HD), F32),
            pltpu.VMEM((NY, 2, 4, 16, HD), BF16),
            pltpu.VMEM((4, 2, NY, 16, HD), BF16),
            pltpu.VMEM((NY, 1, HD), F32),
            pltpu.VMEM((4, NY, 1, HD), F32),
            pltpu.VMEM((2, 2 * HD, D), BF16),
            pltpu.VMEM((CHUNKS, NZ, 16, CW), BF16),
            pltpu.VMEM((CHUNKS, NZ, 16, CW), BF16),
            dma((6,)),
            dma((HEADS,)), dma((HEADS,)), dma((HEADS,)), dma((HEADS,)),
            dma, dma,
            dma((4, NY)), dma((4, NY)),
            dma((4, NX)), dma((4, NX)),
            dma((NY, 4)), dma((NY, 4)), dma((NY, 4)), dma((NY, 4)),
            dma((CHUNKS, NZ)), dma((CHUNKS, NZ)),
        ],
        compiler_params=pltpu.CompilerParams(
            collective_id=0, has_side_effects=True, vmem_limit_bytes=60 * 1024 * 1024
        ),
    )(fresh_query, fresh_entries.transpose(1, 0, 2), cached_entries, recompute_rows, valid_counts.reshape(1, 1), out_weight)
    return (summed[:CAP] * out_gate[None, :]).astype(BF16)


def solution(mesh):
    both = ("head", "blk")
    in_specs = (P(both, None), P(None, both, None), P(None, both, None), P(both, None), P(both), P("head", None), P())
    return jax.shard_map(on_device, mesh=mesh, in_specs=in_specs, out_specs=P(both, None), check_vma=False)
```

time: 408 us -> 54.1 us (0.13)
  waiting for transfers between devices: 246 us -> 0 us
  blocking collectives: 86.9 us -> 0 us
  Pallas kernels: 0 us -> 51.7 us
  local copies, waits for them, and re-layouts: 28.3 us -> 0.01 us
  between operations: 15 us -> 0.68 us
  other arithmetic: 15.8 us -> 1.52 us
  matrix products: 10.3 us -> 0 us
  starting transfers between devices: 4.27 us -> 0 us
    all_gather x1 -> x0, waiting for transfers between devices: 246 us -> none  [on_device(): piece = lax.all_gather(keys_values, 'blk', axis=1, tiled=True)]
    unnamed x1 -> x0, blocking collectives: 54.8 us -> none
    pallas_call x0 -> x1, Pallas kernels: none -> 51.7 us  [on_device(): pl.pallas_call(kernel, out_shape=jax.ShapeDtypeStruct((8, D), F32), in_sp...]
    all_to_all x2 -> x0, blocking collectives: 32.1 us -> none  [the longest x1 20.3 us: on_device(): lax.all_to_all(merged, 'head', split_axis=2, concat_axis=1, tiled=True)]
    slice x3 -> x0, local copies, waits for them, and re-layouts: 18.5 us -> none  [the longest x2 12.1 us: on_device(): key_heads = piece[0].reshape(-1, local_heads, HD)]
    unnamed x1 -> x0, other arithmetic: 11.5 us -> none
    dot_general x4 -> x0, matrix products: 10.3 us -> none  [the longest x1 4.78 us: on_device(): jnp.einsum('qhd,khd->qhk', query_heads, key_heads, preferred_element_type...]
    unnamed x17 -> x2, local copies, waits for them, and re-layouts: 5.92 us -> 0.01 us
  transfers between devices with their start and end apart: 2 -> 0, of which waited for: 2 -> 0; matrix products, arithmetic and copies ran while one was open for 4% -> 0% of each run, Pallas kernels for 0% -> 0%
where the time goes in v3:
time: 54.1 us; the launch traced here: 53.9 us
  Pallas kernels  51.7 us (96%)
  other arithmetic  1.52 us (3%)
  between operations  0.68 us (1%)
    pallas_call x1, Pallas kernels, on_device(): pl.pallas_call(kernel, out_shape=jax.ShapeDtypeStruct((8, D), F32), in_sp...  51.7 us
    convert_element_type x1, other arithmetic, on_device(): return (summed[:CAP] * out_gate[None, :]).astype(BF16)  1.52 us

profile of v3, /device:TPU:1, one launch (start us, length us, event | category | flops | bytes accessed | tf_op | source)
XLA Modules:
  0.0 53.9 jit_solution(2298687452828072050)
XLA Ops:
  0.0 0.0 copy-start
  0.7 51.7 %shard_map.73 = f32[8,3072]{1,0:T(8,128)} custom-call(bf16[7,2048]{1,0:T(8,128)(2,1)} %q_hbm.1, bf16[7,2,2048]{2,1,0:T(2,128)(2,1)} %bitcast.3, bf16[2,16,2048]{2,1,0:T(8,128)(2,1)} %cached_hbm.1, s32[1,7]{1,0:T(1,128)} %rows_hbm.1, s32[1,1]{1,0:T(1,128)} %bitcast.2.cnt_hbm, bf16[256,3072]{1,0:T(8,128)(2,1)} %w_hbm.1), custom_call_target="tpu_custom_call" | custom-call | tf_op jit(solution)/shard_map/pallas_call | solution.py:305
  52.4 0.0 copy-done
  52.4 1.5 %multiply_convert_fusion = bf16[7,3072]{1,0:T(8,128)(2,1)} fusion(f32[8,3072]{1,0:T(8,128)} %shard_map.73, f32[3072]{0:T(1024)S(1)} %copy-done), kind=kLoop, calls=%fused_computation | loop fusion | flops 43008 | bytes 141312 | tf_op jit(solution)/shard_map/convert_element_type | solution.py:344
Async XLA Ops:
  0.0 52.4 %copy-start = (f32[3072]{0:T(1024)S(1)}, f32[3072]{0:T(1024)}, u32[]{:S(2)}) copy-start(f32[3072]{0:T(1024)} %param.13) | copy-start | bytes 36868

commit v4 on v3

v4 whole, which is shorter than its diff:
```python
import functools
import math

import jax
import jax.numpy as jnp
from jax import lax
from jax.experimental import pallas as pl
from jax.experimental.pallas import tpu as pltpu
from jax.sharding import PartitionSpec as P

HD = 128
HEADS = 16
TOK = 16
CAP = 7
D = 3072
NX, NY, NZ, CHIPS = 4, 8, 4, 8
CHUNKS = 3
HALF = D // 2
CW = HALF // CHUNKS
SCALE2 = (HD ** -0.5) * math.log2(math.e)
MESH = pl.DeviceIdType.MESH
F32, BF16 = jnp.float32, jnp.bfloat16

PLACES = [(dz, dc) for dz in range(CHIPS) for dc in range(2)]


def slots(groups):
    return {(dz, dc): g * 4 + dc * 2 + e for g, pair in enumerate(groups) for e, dz in enumerate(pair) for dc in range(2)}


KV_SLOT = slots(((1, 7), (2, 6), (3, 5), (0, 4)))
Q_SLOT = slots(((1, 5), (3, 7), (0, 4), (2, 6)))
NEAR_FIRST = sorted((k for k in PLACES if k != (0, 0)), key=lambda k: min(k[0], CHIPS - k[0]))
FAR_FIRST = NEAR_FIRST[::-1]
ORDER = (4, 3, 5, 2, 6, 1, 7, 0)


def kernel(
    q_hbm, fresh_hbm, cached_hbm, rows_hbm, cnt_hbm, w_hbm, out_ref,
    q_in, fresh_in, cached_in, rows_in, cnt_in, fresh32, q_out, kv_out, q_land, kv_all, q_all, vt,
    top_ref, mix_ref, o_out, o_in, st_out, st_in, w_all, p_out, p_in,
    sem_in, qz_s, qz_r, kz_s, kz_r, w_s, w_r, qy_s, qy_r, kx_s, kx_r, o_s, o_r, t_s, t_r, p_s, p_r,
):
    head = lax.axis_index("head")
    blk = lax.axis_index("blk")

    def div(a, b):
        return lax.div(a, jnp.int32(b))

    def rem(a, b):
        return lax.rem(a, jnp.int32(b))

    core, zh = rem(head, 2), div(head, 2)
    y, zl, x = rem(blk, NY), rem(div(blk, NY), 2), div(blk, 2 * NY)
    chip = zh * 2 + zl
    ups = [rem(chip + dz, CHIPS) for dz in range(CHIPS)]
    cores = [core, 1 - core]

    def at_z(dz, dc):
        return (div(ups[dz], 2) * 2 + cores[dc], (x * 2 + rem(ups[dz], 2)) * NY + y)

    def head_of(dz, dc):
        return div(ups[dz], 2) * 4 + cores[dc] * 2 + rem(ups[dz], 2)

    def at_x(dx):
        return (head, (rem(x + dx, NX) * 2 + zl) * NY + y)

    def at_y(dy):
        return (head, (x * 2 + zl) * NY + rem(y + dy, NY))

    def at_o(dy, odd, dc):
        return (zh * 2 + cores[dc], (x * 2 + (1 - zl if odd else zl)) * NY + rem(y + dy, NY))

    def at_p(b):
        return (rem(zh + b, NZ) * 2 + core, blk)

    def send(src, dst, s_sem, r_sem, dev):
        return pltpu.make_async_remote_copy(
            src_ref=src, dst_ref=dst, send_sem=s_sem, recv_sem=r_sem,
            device_id=dev, device_id_type=MESH,
        )

    def arrived(ref, sem):
        send(ref, ref, sem, sem, at_x(1)).wait_recv()

    def left(ref, sem):
        send(ref, ref, sem, sem, at_x(1)).wait_send()

    loads = [
        pltpu.make_async_copy(q_hbm, q_in, sem_in.at[0]),
        pltpu.make_async_copy(fresh_hbm, fresh_in, sem_in.at[1]),
        pltpu.make_async_copy(cached_hbm, cached_in, sem_in.at[2]),
        pltpu.make_async_copy(rows_hbm, rows_in, sem_in.at[3]),
        pltpu.make_async_copy(cnt_hbm, cnt_in, sem_in.at[4]),
        pltpu.make_async_copy(w_hbm, w_all.at[0], sem_in.at[5]),
    ]
    barrier = pltpu.get_barrier_semaphore()
    partners = [at_z(dz, dc) for dz, dc in FAR_FIRST]
    partners += [at_y(dy) for dy in ORDER[:7]] + [at_x(dx) for dx in (2, 1, 3)]
    for dev in partners:
        pl.semaphore_signal(barrier, inc=1, device_id=dev, device_id_type=MESH)
    for load in loads[:5]:
        load.start()

    fresh32[0, ...] = jnp.zeros((8, HEADS * HD), F32)
    loads[0].wait()
    fresh32[0, 0:CAP, :] = q_in[...].astype(F32)

    def lanes(h):
        return pl.ds(pl.multiple_of(h * HD, HD), HD)

    for place in [(0, 0)] + FAR_FIRST:
        rows8 = fresh32[0, :, lanes(head_of(*place))]
        q_out[Q_SLOT[place]] = jnp.concatenate([rows8, jnp.zeros((8, HD), F32)], axis=0).astype(BF16)
    q_land[Q_SLOT[0, 0]] = q_out[Q_SLOT[0, 0]]
    pl.semaphore_wait(barrier, len(partners))

    def z_send(out, land, s_sem, r_sem, table, place):
        back = table[(CHIPS - place[0]) % CHIPS, place[1]]
        send(out.at[table[place]], land.at[back], s_sem, r_sem.at[back // 4], at_z(*place)).start()

    for place in FAR_FIRST:
        z_send(q_out, q_land, qz_s, qz_r, Q_SLOT, place)

    for i in (1, 2, 3, 4):
        loads[i].wait()
    for i in range(2):
        fresh32[1 + i, 0:CAP, :] = fresh_in[:, i, :].astype(F32)
    count = cnt_in[0, 0]
    token = lax.broadcasted_iota(jnp.int32, (TOK, HD), 0)
    hits = []
    for c in range(CAP):
        used = jnp.full((TOK, HD), c, jnp.int32) < count
        hits.append((token == rows_in[0, c]) & used)

    def merged(h, i):
        rows = cached_in[i, :, lanes(h)].astype(F32)
        for c in range(CAP):
            rows = jnp.where(hits[c], fresh32[1 + i, c:c + 1, lanes(h)], rows)
        return rows.astype(BF16)

    for place in NEAR_FIRST:
        for i in range(2):
            kv_out[KV_SLOT[place], i * TOK:(i + 1) * TOK, :] = merged(head_of(*place), i)
        z_send(kv_out, kv_all.at[0], kz_s, kz_r, KV_SLOT, place)
    for i in range(2):
        kv_all[0, KV_SLOT[0, 0], i * TOK:(i + 1) * TOK, :] = merged(head_of(0, 0), i)

    loads[5].start()
    send(w_hbm, w_all.at[1], w_s, w_r, at_z(0, 1)).start()

    for t, half in enumerate((zl, 1 - zl, 0, 1)):
        first = t * 4 + (t * 4 == Q_SLOT[0, 0])
        arrived(q_land.at[first:t * 4 + 4], qz_r.at[t])
        packed = q_land[t * 4:(t + 1) * 4].astype(F32)[:, 0:8, :].reshape(32, HD)
        part = slice(t // 2 * 32, t // 2 * 32 + 32)
        q_all[half, 7, part, :] = packed.astype(BF16)
        for p in range(7):
            send(
                q_all.at[half, 7, part], q_all.at[half, p, part], qy_s, qy_r.at[p // 4], at_y(ORDER[p])
            ).start()
    for g in range(4):
        first = g * 4 + (g * 4 == KV_SLOT[0, 0])
        arrived(kv_all.at[0, first:g * 4 + 4], kz_r.at[g])
        part = slice(g * 4, g * 4 + 4)
        for s in (2, 1, 3):
            send(kv_all.at[0, part], kv_all.at[s, part], kx_s, kx_r.at[g], at_x(s)).start()

    tokens = NX * 4 * TOK
    vt[HD:HD + 16, :] = jnp.ones((16, tokens), BF16)

    def attend(keys, unit, first):
        queries = q_all[unit // 2, unit % 2 * 4:unit % 2 * 4 + 4].reshape(2 * HD, HD)
        scores = lax.dot_general(keys, queries, (((1,), (1,)), ((), ())), preferred_element_type=F32)
        top = jnp.max(scores, axis=0, keepdims=True) * SCALE2
        if not first:
            old = top_ref[unit]
            top = jnp.maximum(top, old)
        weights = jnp.exp2(scores * SCALE2 - top).astype(BF16)
        mixed = jnp.dot(vt[...], weights, preferred_element_type=F32)
        if not first:
            mixed = mixed + mix_ref[unit] * jnp.exp2(old - top)
        return top, mixed

    def own(p, g):
        return p == 7 and g == 2

    for g in range(4):
        part = slice(g * 4, g * 4 + 4)
        arrived(kv_all.at[1:4, part], kx_r.at[g])
        keys = kv_all[:, part, 0:TOK, :].reshape(tokens, HD)
        vt[0:HD, :] = kv_all[:, part, TOK:2 * TOK, :].reshape(tokens, HD).astype(F32).T.astype(BF16)
        for unit in (1, 3, 0, 2) if g == 0 else (0, 1, 2, 3):
            if g == 0 and unit == 1:
                arrived(q_all.at[:, 4:7], qy_r.at[1])
            if g == 0 and unit == 0:
                arrived(q_all.at[:, 0:4], qy_r.at[0])
            top, mixed = attend(keys, unit, g == 0)
            if g < 3:
                top_ref[unit] = top
                mix_ref[unit] = mixed
                continue
            i, base = unit // 2, unit % 2 * 4
            total = mixed[HD:HD + 1, :]
            level = top + jnp.log2(total)
            rows = (mixed[0:HD, :] * (1.0 / total)).T.astype(BF16)
            for n in range(2):
                st_out[i, base // 2 + n] = level[:, n * HD:(n + 1) * HD]
            o_out[i, base:base + 4] = rows.reshape(4, 64, HD)
            for p in range(base, base + 4):
                for k in range(4):
                    if not own(p, k):
                        dev = at_o(NY - ORDER[p], k < 2, k % 2)
                        send(st_out.at[i, p // 2], st_in.at[i, k, p], t_s.at[i, k], t_r.at[i, k], dev).start()
                        piece = o_out.at[i, p, k * 16:(k + 1) * 16]
                        send(piece, o_in.at[i, k, p], o_s.at[i, k], o_r.at[i, k], dev).start()

    row8 = lax.broadcasted_iota(jnp.int32, (8, HD), 0)
    lane8 = lax.broadcasted_iota(jnp.int32, (8, HD), 1)
    row = lax.broadcasted_iota(jnp.int32, (16, HD), 0)
    lane = lax.broadcasted_iota(jnp.int32, (16, HD), 1)
    straight = rem(lane, 16) == row
    swapped = rem(lane, 16) == rem(row + 8, 16)
    valid = lax.broadcasted_iota(jnp.int32, (8, CW), 0) < count
    for i in range(2):
        st_in[i, 2, 7] = st_out[i, 3]
        o_in[i, 2, 7] = o_out[i, 7, 32:48]
        levels = []
        for k in range(4):
            arrived(st_in.at[i, k, 0:8 - (k == 2)], t_r.at[i, k])
            seen = jnp.concatenate([st_in[i, k, p] for p in range(NY)], axis=0)
            seen = pltpu.roll(seen, 0, 1, stride=16, stride_axis=0)
            low, high = (pltpu.roll(seen, (HD + shift - k * 16) % HD, 1) for shift in (0, 64))
            moved = jnp.where(rem(row8, 2) == 0, low, high)
            levels.append(jnp.sum(jnp.where(div(lane8, 16) == row8, moved, 0.0), axis=0, keepdims=True))
        levels = jnp.concatenate(levels + levels, axis=0)
        peak = levels
        for shift in (16, 32, 64):
            peak = jnp.maximum(peak, pltpu.roll(peak, shift, 1))
        parts = jnp.exp2(levels - peak)
        total = parts
        for shift in (16, 32, 64):
            total = total + pltpu.roll(total, shift, 1)
        shares = parts / total

        mean = []
        for k in range(4):
            arrived(o_in.at[i, k, 0:8 - (k == 2)], o_r.at[i, k])
            mix = jnp.where(straight, shares[k:k + 1, :], 0.0)
            if k < 2 and i == 0:
                mix = jnp.where(zl == 1, mix, jnp.where(swapped, shares[k:k + 1, :], 0.0))
            mean.append(jnp.dot(mix.astype(BF16), o_in[i, k].reshape(HD, HD), preferred_element_type=F32))
        heads4 = [jnp.where(zl == z, mean[2 + dc], mean[dc]) for dc in range(2) for z in range(2)]
        rows = jnp.concatenate(heads4, axis=1).astype(BF16)

        if i == 0:
            loads[5].wait()
            send(w_hbm, w_all.at[1], w_s, w_r, at_z(0, 1)).wait_recv()
        for ci in range(CHUNKS):
            sides = []
            for start in (ci * CW, HALF + ci * CW):
                w = jnp.concatenate([w_all[0, :, start:start + CW], w_all[1, :, start:start + CW]], axis=0)
                sides.append(jnp.dot(rows, w, preferred_element_type=F32))
            for n in range(2):
                b = n * 2 + i
                block = jnp.concatenate([side[n * 8:(n + 1) * 8] for side in sides], axis=0)
                p_out[b, ci] = block.astype(BF16)
                if b:
                    send(p_out.at[b, ci], p_in.at[b, ci], p_s.at[b], p_r.at[b], at_p(b)).start()

    for b in (2, 1, 3):
        arrived(p_in.at[b], p_r.at[b])
    for ci in range(CHUNKS):
        total = p_out[0, ci].astype(F32)
        for b in (1, 3, 2):
            total = total + p_in[b, ci].astype(F32)
        out_ref[:, ci * CW:(ci + 1) * CW] = jnp.where(valid, total[0:8], 0.0)
        out_ref[:, HALF + ci * CW:HALF + (ci + 1) * CW] = jnp.where(valid, total[8:16], 0.0)

    left(q_out.at[0:15], qz_s)
    left(kv_out.at[0:15], kz_s)
    send(w_hbm, w_all.at[1], w_s, w_r, at_z(0, 1)).wait_send()
    left(q_all.at[:, 0:7], qy_s)
    left(kv_all.at[1:4], kx_s)
    for i in range(2):
        for k in range(4):
            left(st_in.at[i, k, 0:8 - (k == 2)], t_s.at[i, k])
            left(o_in.at[i, k, 0:8 - (k == 2)], o_s.at[i, k])
    for b in range(1, NZ):
        left(p_out.at[b], p_s.at[b])


def on_device(fresh_query, fresh_entries, cached_entries, recompute_rows, valid_counts, out_weight, out_gate):
    dma = pltpu.SemaphoreType.DMA
    width = HEADS * HD
    summed = pl.pallas_call(
        kernel,
        out_shape=pltpu.VMEM((8, D), F32),
        in_specs=[pl.BlockSpec(memory_space=pl.ANY)] * 6,
        out_specs=pl.BlockSpec(memory_space=pltpu.VMEM),
        scratch_shapes=[
            pltpu.VMEM((CAP, width), BF16),
            pltpu.VMEM((CAP, 2, width), BF16),
            pltpu.VMEM((2, TOK, width), BF16),
            pltpu.SMEM((1, CAP), jnp.int32),
            pltpu.SMEM((1, 1), jnp.int32),
            pltpu.VMEM((3, 8, width), F32),
            pltpu.VMEM((HEADS, 16, HD), BF16),
            pltpu.VMEM((HEADS, 2 * TOK, HD), BF16),
            pltpu.VMEM((HEADS, 16, HD), BF16),
            pltpu.VMEM((NX, HEADS, 2 * TOK, HD), BF16),
            pltpu.VMEM((2, NY, 64, HD), BF16),
            pltpu.VMEM((HD + 16, HEADS * TOK), BF16),
            pltpu.VMEM((4, 1, 2 * HD), F32),
            pltpu.VMEM((4, HD + 16, 2 * HD), F32),
            pltpu.VMEM((2, NY, 64, HD), BF16),
            pltpu.VMEM((2, 4, NY, 16, HD), BF16),
            pltpu.VMEM((2, 4, 1, HD), F32),
            pltpu.VMEM((2, 4, NY, 1, HD), F32),
            pltpu.VMEM((2, 2 * HD, D), BF16),
            pltpu.VMEM((NZ, CHUNKS, 16, CW), BF16),
            pltpu.VMEM((NZ, CHUNKS, 16, CW), BF16),
            dma((6,)),
            dma, dma((4,)), dma, dma((4,)),
            dma, dma,
            dma, dma((2,)),
            dma, dma((4,)),
            dma((2, 4)), dma((2, 4)), dma((2, 4)), dma((2, 4)),
            dma((NZ,)), dma((NZ,)),
        ],
        compiler_params=pltpu.CompilerParams(
            collective_id=0, has_side_effects=True, vmem_limit_bytes=60 * 1024 * 1024
        ),
    )(fresh_query, fresh_entries.transpose(1, 0, 2), cached_entries, recompute_rows, valid_counts.reshape(1, 1), out_weight)
    return (summed[:CAP] * out_gate[None, :]).astype(BF16)


def solution(mesh):
    both = ("head", "blk")
    in_specs = (P(both, None), P(None, both, None), P(None, both, None), P(both, None), P(both), P("head", None), P())
    return jax.shard_map(on_device, mesh=mesh, in_specs=in_specs, out_specs=P(both, None), check_vma=False)
```

time: 54.1 us -> 49.5 us (0.915)
  Pallas kernels: 51.7 us -> 48.1 us
  other arithmetic: 1.52 us -> 0.63 us
    pallas_call x1, Pallas kernels: 51.7 us -> 48.1 us  [on_device(): pl.pallas_call(kernel, out_shape=pltpu.VMEM((8, D), F32), in_specs=[pl.Bl...]
    convert_element_type x1, other arithmetic: 1.52 us -> 0.63 us  [on_device(): return (summed[:CAP] * out_gate[None, :]).astype(BF16)]
where the time goes in v4:
time: 49.5 us; the launch traced here: 49.4 us
  Pallas kernels  48.1 us (97%)
  between operations  0.68 us (1%)
  other arithmetic  0.63 us (1%)
    pallas_call x1, Pallas kernels, on_device(): pl.pallas_call(kernel, out_shape=pltpu.VMEM((8, D), F32), in_specs=[pl.Bl...  48.1 us

profile of v4, /device:TPU:1, one launch (start us, length us, event | category | flops | bytes accessed | tf_op | source)
XLA Modules:
  0.0 49.4 jit_solution(1072765616184365363)
XLA Ops:
  0.0 0.0 copy-start
  0.7 48.1 %shard_map.73 = f32[8,3072]{1,0:T(8,128)S(1)} custom-call(bf16[7,2048]{1,0:T(8,128)(2,1)} %q_hbm.1, bf16[7,2,2048]{2,1,0:T(2,128)(2,1)} %bitcast.3, bf16[2,16,2048]{2,1,0:T(8,128)(2,1)} %cached_hbm.1, s32[1,7]{1,0:T(1,128)} %rows_hbm.1, s32[1,1]{1,0:T(1,128)} %bitcast.2.cnt_hbm, bf16[256,3072]{1,0:T(8,128)(2,1)} %w_hbm.1), custom_call_target="tpu_custom_call" | custom-call | tf_op jit(solution)/shard_map/pallas_call | solution.py:296
  48.7 0.0 copy-done
  48.7 0.6 %multiply_convert_fusion = bf16[7,3072]{1,0:T(8,128)(2,1)} fusion(f32[8,3072]{1,0:T(8,128)S(1)} %shard_map.73, f32[3072]{0:T(1024)S(1)} %copy-done), kind=kLoop, calls=%fused_computation | loop fusion | flops 43008 | bytes 141312 | tf_op jit(solution)/shard_map/convert_element_type | solution.py:335
Async XLA Ops:
  0.0 48.7 %copy-start = (f32[3072]{0:T(1024)S(1)}, f32[3072]{0:T(1024)}, u32[]{:S(2)}) copy-start(f32[3072]{0:T(1024)} %param.13) | copy-start | bytes 36868

commit v5 on v4

--- a/solution.py
+++ b/solution.py
@@ -38,7 +38,7 @@
 def kernel(
     q_hbm, fresh_hbm, cached_hbm, rows_hbm, cnt_hbm, w_hbm, out_ref,
     q_in, fresh_in, cached_in, rows_in, cnt_in, fresh32, q_out, kv_out, q_land, kv_all, q_all, vt,
-    top_ref, mix_ref, o_out, o_in, st_out, st_in, w_all, p_out, p_in,
+    o_out, o_in, st_out, st_in, w_all, p_out, p_in,
     sem_in, qz_s, qz_r, kz_s, kz_r, w_s, w_r, qy_s, qy_r, kx_s, kx_r, o_s, o_r, t_s, t_r, p_s, p_r,
 ):
     head = lax.axis_index("head")
@@ -149,7 +149,8 @@
     loads[5].start()
     send(w_hbm, w_all.at[1], w_s, w_r, at_z(0, 1)).start()
 
-    for t, half in enumerate((zl, 1 - zl, 0, 1)):
+    def pass_queries(t):
+        half = (zl, 1 - zl, 0, 1)[t]
         first = t * 4 + (t * 4 == Q_SLOT[0, 0])
         arrived(q_land.at[first:t * 4 + 4], qz_r.at[t])
         packed = q_land[t * 4:(t + 1) * 4].astype(F32)[:, 0:8, :].reshape(32, HD)
@@ -159,61 +160,59 @@
             send(
                 q_all.at[half, 7, part], q_all.at[half, p, part], qy_s, qy_r.at[p // 4], at_y(ORDER[p])
             ).start()
-    for g in range(4):
+
+    def pass_entries(g):
         first = g * 4 + (g * 4 == KV_SLOT[0, 0])
         arrived(kv_all.at[0, first:g * 4 + 4], kz_r.at[g])
         part = slice(g * 4, g * 4 + 4)
         for s in (2, 1, 3):
             send(kv_all.at[0, part], kv_all.at[s, part], kx_s, kx_r.at[g], at_x(s)).start()
 
-    tokens = NX * 4 * TOK
-    vt[HD:HD + 16, :] = jnp.ones((16, tokens), BF16)
-
-    def attend(keys, unit, first):
+    pass_queries(3)
+    pass_entries(0)
+    pass_queries(0)
+    pass_queries(1)
+    pass_entries(1)
+    pass_entries(2)
+    pass_queries(2)
+    pass_entries(3)
+
+    group = NX * 4 * TOK
+    for g in range(4):
+        part = slice(g * 4, g * 4 + 4)
+        arrived(kv_all.at[1:4, part], kx_r.at[g])
+        values = kv_all[:, part, TOK:2 * TOK, :].reshape(group, HD)
+        vt[0:HD, g * group:(g + 1) * group] = values.astype(F32).T.astype(BF16)
+    vt[HD:HD + 16, :] = jnp.ones((16, 4 * group), BF16)
+
+    def own(p, g):
+        return p == 7 and g == 2
+
+    for near in (1, 0):
+        arrived(q_all.at[:, near * 4:near * 4 + 4 - near], qy_r.at[near])
+    for unit in range(4):
+        keys = jnp.concatenate(
+            [kv_all[:, g * 4:g * 4 + 4, 0:TOK, :].reshape(group, HD) for g in range(4)], axis=0
+        )
         queries = q_all[unit // 2, unit % 2 * 4:unit % 2 * 4 + 4].reshape(2 * HD, HD)
         scores = lax.dot_general(keys, queries, (((1,), (1,)), ((), ())), preferred_element_type=F32)
         top = jnp.max(scores, axis=0, keepdims=True) * SCALE2
-        if not first:
-            old = top_ref[unit]
-            top = jnp.maximum(top, old)
         weights = jnp.exp2(scores * SCALE2 - top).astype(BF16)
         mixed = jnp.dot(vt[...], weights, preferred_element_type=F32)
-        if not first:
-            mixed = mixed + mix_ref[unit] * jnp.exp2(old - top)
-        return top, mixed
-
-    def own(p, g):
-        return p == 7 and g == 2
-
-    for g in range(4):
-        part = slice(g * 4, g * 4 + 4)
-        arrived(kv_all.at[1:4, part], kx_r.at[g])
-        keys = kv_all[:, part, 0:TOK, :].reshape(tokens, HD)
-        vt[0:HD, :] = kv_all[:, part, TOK:2 * TOK, :].reshape(tokens, HD).astype(F32).T.astype(BF16)
-        for unit in (1, 3, 0, 2) if g == 0 else (0, 1, 2, 3):
-            if g == 0 and unit == 1:
-                arrived(q_all.at[:, 4:7], qy_r.at[1])
-            if g == 0 and unit == 0:
-                arrived(q_all.at[:, 0:4], qy_r.at[0])
-            top, mixed = attend(keys, unit, g == 0)
-            if g < 3:
-                top_ref[unit] = top
-                mix_ref[unit] = mixed
-                continue
-            i, base = unit // 2, unit % 2 * 4
-            total = mixed[HD:HD + 1, :]
-            level = top + jnp.log2(total)
-            rows = (mixed[0:HD, :] * (1.0 / total)).T.astype(BF16)
-            for n in range(2):
-                st_out[i, base // 2 + n] = level[:, n * HD:(n + 1) * HD]
-            o_out[i, base:base + 4] = rows.reshape(4, 64, HD)
-            for p in range(base, base + 4):
-                for k in range(4):
-                    if not own(p, k):
-                        dev = at_o(NY - ORDER[p], k < 2, k % 2)
-                        send(st_out.at[i, p // 2], st_in.at[i, k, p], t_s.at[i, k], t_r.at[i, k], dev).start()
-                        piece = o_out.at[i, p, k * 16:(k + 1) * 16]
-                        send(piece, o_in.at[i, k, p], o_s.at[i, k], o_r.at[i, k], dev).start()
+        i, base = unit // 2, unit % 2 * 4
+        total = mixed[HD:HD + 1, :]
+        level = top + jnp.log2(total)
+        rows = (mixed[0:HD, :] * (1.0 / total)).T.astype(BF16)
+        for n in range(2):
+            st_out[i, base // 2 + n] = level[:, n * HD:(n + 1) * HD]
+        o_out[i, base:base + 4] = rows.reshape(4, 64, HD)
+        for p in range(base, base + 4):
+            for k in range(4):
+                if not own(p, k):
+                    dev = at_o(NY - ORDER[p], k < 2, k % 2)
+                    send(st_out.at[i, p // 2], st_in.at[i, k, p], t_s.at[i, k], t_r.at[i, k], dev).start()
+                    piece = o_out.at[i, p, k * 16:(k + 1) * 16]
+                    send(piece, o_in.at[i, k, p], o_s.at[i, k], o_r.at[i, k], dev).start()
 
     row8 = lax.broadcasted_iota(jnp.int32, (8, HD), 0)
     lane8 = lax.broadcasted_iota(jnp.int32, (8, HD), 1)
@@ -310,9 +309,7 @@
             pltpu.VMEM((HEADS, 16, HD), BF16),
             pltpu.VMEM((NX, HEADS, 2 * TOK, HD), BF16),
             pltpu.VMEM((2, NY, 64, HD), BF16),
-            pltpu.VMEM((HD + 16, HEADS * TOK), BF16),
-            pltpu.VMEM((4, 1, 2 * HD), F32),
-            pltpu.VMEM((4, HD + 16, 2 * HD), F32),
+            pltpu.VMEM((HD + 16, 4 * HEADS * TOK), BF16),
             pltpu.VMEM((2, NY, 64, HD), BF16),
             pltpu.VMEM((2, 4, NY, 16, HD), BF16),
             pltpu.VMEM((2, 4, 1, HD), F32),

time: 49.5 us -> 47 us (0.949)
  Pallas kernels: 48.1 us -> 45.5 us
    pallas_call x1, Pallas kernels: 48.1 us -> 45.5 us  [on_device(): pl.pallas_call(kernel, out_shape=pltpu.VMEM((8, D), F32), in_specs=[pl.Bl...]
where the time goes in v5:
time: 47 us; the launch traced here: 46.8 us
  Pallas kernels  45.5 us (97%)
  between operations  0.68 us (1%)
  other arithmetic  0.63 us (1%)
    pallas_call x1, Pallas kernels, on_device(): pl.pallas_call(kernel, out_shape=pltpu.VMEM((8, D), F32), in_specs=[pl.Bl...  45.5 us

profile of v5, /device:TPU:1, one launch (start us, length us, event | category | flops | bytes accessed | tf_op | source)
XLA Modules:
  0.0 46.8 jit_solution(12240759635374533100)
XLA Ops:
  0.0 0.0 copy-start
  0.7 45.5 %shard_map.73 = f32[8,3072]{1,0:T(8,128)S(1)} custom-call(bf16[7,2048]{1,0:T(8,128)(2,1)} %q_hbm.1, bf16[7,2,2048]{2,1,0:T(2,128)(2,1)} %bitcast.3, bf16[2,16,2048]{2,1,0:T(8,128)(2,1)} %cached_hbm.1, s32[1,7]{1,0:T(1,128)} %rows_hbm.1, s32[1,1]{1,0:T(1,128)} %bitcast.2.cnt_hbm, bf16[256,3072]{1,0:T(8,128)(2,1)} %w_hbm.1), custom_call_target="tpu_custom_call" | custom-call | tf_op jit(solution)/shard_map/pallas_call | solution.py:295
  46.2 0.0 copy-done
  46.2 0.6 %multiply_convert_fusion = bf16[7,3072]{1,0:T(8,128)(2,1)} fusion(f32[8,3072]{1,0:T(8,128)S(1)} %shard_map.73, f32[3072]{0:T(1024)S(1)} %copy-done), kind=kLoop, calls=%fused_computation | loop fusion | flops 43008 | bytes 141312 | tf_op jit(solution)/shard_map/convert_element_type | solution.py:332
Async XLA Ops:
  0.0 46.2 %copy-start = (f32[3072]{0:T(1024)S(1)}, f32[3072]{0:T(1024)}, u32[]{:S(2)}) copy-start(f32[3072]{0:T(1024)} %param.13) | copy-start | bytes 36868

commit v6 on v5

--- a/solution.py
+++ b/solution.py
@@ -97,10 +97,12 @@
     barrier = pltpu.get_barrier_semaphore()
     partners = [at_z(dz, dc) for dz, dc in FAR_FIRST]
     partners += [at_y(dy) for dy in ORDER[:7]] + [at_x(dx) for dx in (2, 1, 3)]
-    for dev in partners:
+    for dev in partners[:15]:
         pl.semaphore_signal(barrier, inc=1, device_id=dev, device_id_type=MESH)
     for load in loads[:5]:
         load.start()
+    for dev in partners[15:]:
+        pl.semaphore_signal(barrier, inc=1, device_id=dev, device_id_type=MESH)
 
     fresh32[0, ...] = jnp.zeros((8, HEADS * HD), F32)
     loads[0].wait()
@@ -113,14 +115,10 @@
         rows8 = fresh32[0, :, lanes(head_of(*place))]
         q_out[Q_SLOT[place]] = jnp.concatenate([rows8, jnp.zeros((8, HD), F32)], axis=0).astype(BF16)
     q_land[Q_SLOT[0, 0]] = q_out[Q_SLOT[0, 0]]
-    pl.semaphore_wait(barrier, len(partners))
 
     def z_send(out, land, s_sem, r_sem, table, place):
         back = table[(CHIPS - place[0]) % CHIPS, place[1]]
         send(out.at[table[place]], land.at[back], s_sem, r_sem.at[back // 4], at_z(*place)).start()
-
-    for place in FAR_FIRST:
-        z_send(q_out, q_land, qz_s, qz_r, Q_SLOT, place)
 
     for i in (1, 2, 3, 4):
         loads[i].wait()
@@ -139,12 +137,16 @@
             rows = jnp.where(hits[c], fresh32[1 + i, c:c + 1, lanes(h)], rows)
         return rows.astype(BF16)
 
-    for place in NEAR_FIRST:
+    for place in PLACES:
         for i in range(2):
             kv_out[KV_SLOT[place], i * TOK:(i + 1) * TOK, :] = merged(head_of(*place), i)
+    kv_all[0, KV_SLOT[0, 0]] = kv_out[KV_SLOT[0, 0]]
+
+    pl.semaphore_wait(barrier, len(partners))
+    for place in FAR_FIRST:
+        z_send(q_out, q_land, qz_s, qz_r, Q_SLOT, place)
+    for place in NEAR_FIRST:
         z_send(kv_out, kv_all.at[0], kz_s, kz_r, KV_SLOT, place)
-    for i in range(2):
-        kv_all[0, KV_SLOT[0, 0], i * TOK:(i + 1) * TOK, :] = merged(head_of(0, 0), i)
 
     loads[5].start()
     send(w_hbm, w_all.at[1], w_s, w_r, at_z(0, 1)).start()
@@ -211,6 +213,10 @@
                 if not own(p, k):
                     dev = at_o(NY - ORDER[p], k < 2, k % 2)
                     send(st_out.at[i, p // 2], st_in.at[i, k, p], t_s.at[i, k], t_r.at[i, k], dev).start()
+        for p in range(base, base + 4):
+            for k in range(4):
+                if not own(p, k):
+                    dev = at_o(NY - ORDER[p], k < 2, k % 2)
                     piece = o_out.at[i, p, k * 16:(k + 1) * 16]
                     send(piece, o_in.at[i, k, p], o_s.at[i, k], o_r.at[i, k], dev).start()
 

time: 47 us -> 46.2 us (0.983)
  Pallas kernels: 45.5 us -> 44.7 us
    pallas_call x1, Pallas kernels: 45.5 us -> 44.7 us  [on_device(): pl.pallas_call(kernel, out_shape=pltpu.VMEM((8, D), F32), in_specs=[pl.Bl...]
where the time goes in v6:
time: 46.2 us; the launch traced here: 46 us
  Pallas kernels  44.7 us (97%)
  between operations  0.68 us (1%)
  other arithmetic  0.63 us (1%)
    pallas_call x1, Pallas kernels, on_device(): pl.pallas_call(kernel, out_shape=pltpu.VMEM((8, D), F32), in_specs=[pl.Bl...  44.7 us

profile of v6, /device:TPU:1, one launch (start us, length us, event | category | flops | bytes accessed | tf_op | source)
XLA Modules:
  0.0 46.0 jit_solution(14750153573581508730)
XLA Ops:
  0.0 0.0 copy-start
  0.7 44.7 %shard_map.73 = f32[8,3072]{1,0:T(8,128)S(1)} custom-call(bf16[7,2048]{1,0:T(8,128)(2,1)} %q_hbm.1, bf16[7,2,2048]{2,1,0:T(2,128)(2,1)} %bitcast.3, bf16[2,16,2048]{2,1,0:T(8,128)(2,1)} %cached_hbm.1, s32[1,7]{1,0:T(1,128)} %rows_hbm.1, s32[1,1]{1,0:T(1,128)} %bitcast.2.cnt_hbm, bf16[256,3072]{1,0:T(8,128)(2,1)} %w_hbm.1), custom_call_target="tpu_custom_call" | custom-call | tf_op jit(solution)/shard_map/pallas_call | solution.py:301
  45.3 0.0 copy-done
  45.4 0.6 %multiply_convert_fusion = bf16[7,3072]{1,0:T(8,128)(2,1)} fusion(f32[8,3072]{1,0:T(8,128)S(1)} %shard_map.73, f32[3072]{0:T(1024)S(1)} %copy-done), kind=kLoop, calls=%fused_computation | loop fusion | flops 43008 | bytes 141312 | tf_op jit(solution)/shard_map/convert_element_type | solution.py:338
Async XLA Ops:
  0.0 45.4 %copy-start = (f32[3072]{0:T(1024)S(1)}, f32[3072]{0:T(1024)}, u32[]{:S(2)}) copy-start(f32[3072]{0:T(1024)} %param.13) | copy-start | bytes 36868

commit v7 on v6

--- a/solution.py
+++ b/solution.py
@@ -13,7 +13,7 @@
 TOK = 16
 CAP = 7
 D = 3072
-NX, NY, NZ, CHIPS = 4, 8, 4, 8
+NX, NY, CHIPS = 4, 8, 8
 CHUNKS = 3
 HALF = D // 2
 CW = HALF // CHUNKS
@@ -28,8 +28,8 @@
     return {(dz, dc): g * 4 + dc * 2 + e for g, pair in enumerate(groups) for e, dz in enumerate(pair) for dc in range(2)}
 
 
-KV_SLOT = slots(((1, 7), (2, 6), (3, 5), (0, 4)))
-Q_SLOT = slots(((1, 5), (3, 7), (0, 4), (2, 6)))
+SLOT = slots(((1, 7), (2, 6), (3, 5), (0, 4)))
+SELF = SLOT[0, 0]
 NEAR_FIRST = sorted((k for k in PLACES if k != (0, 0)), key=lambda k: min(k[0], CHIPS - k[0]))
 FAR_FIRST = NEAR_FIRST[::-1]
 ORDER = (4, 3, 5, 2, 6, 1, 7, 0)
@@ -37,7 +37,7 @@
 
 def kernel(
     q_hbm, fresh_hbm, cached_hbm, rows_hbm, cnt_hbm, w_hbm, out_ref,
-    q_in, fresh_in, cached_in, rows_in, cnt_in, fresh32, q_out, kv_out, q_land, kv_all, q_all, vt,
+    q_in, fresh_in, cached_in, rows_in, cnt_in, fresh32, q_out, kv_out, q_land, kv_all, q_row, q_all, vt,
     o_out, o_in, st_out, st_in, w_all, p_out, p_in,
     sem_in, qz_s, qz_r, kz_s, kz_r, w_s, w_r, qy_s, qy_r, kx_s, kx_r, o_s, o_r, t_s, t_r, p_s, p_r,
 ):
@@ -53,6 +53,9 @@
     core, zh = rem(head, 2), div(head, 2)
     y, zl, x = rem(blk, NY), rem(div(blk, NY), 2), div(blk, 2 * NY)
     chip = zh * 2 + zl
+    cube, mine = div(zh, 2), rem(zh, 2)
+    quarter = zl * 2 + core
+    place_here = cube * 8 + quarter * 2 + mine
     ups = [rem(chip + dz, CHIPS) for dz in range(CHIPS)]
     cores = [core, 1 - core]
 
@@ -71,8 +74,8 @@
     def at_o(dy, odd, dc):
         return (zh * 2 + cores[dc], (x * 2 + (1 - zl if odd else zl)) * NY + rem(y + dy, NY))
 
-    def at_p(b):
-        return (rem(zh + b, NZ) * 2 + core, blk)
+    def at_p(half, n):
+        return ((half * 2 + n) * 2 + core, blk)
 
     def send(src, dst, s_sem, r_sem, dev):
         return pltpu.make_async_remote_copy(
@@ -113,12 +116,13 @@
 
     for place in [(0, 0)] + FAR_FIRST:
         rows8 = fresh32[0, :, lanes(head_of(*place))]
-        q_out[Q_SLOT[place]] = jnp.concatenate([rows8, jnp.zeros((8, HD), F32)], axis=0).astype(BF16)
-    q_land[Q_SLOT[0, 0]] = q_out[Q_SLOT[0, 0]]
-
-    def z_send(out, land, s_sem, r_sem, table, place):
-        back = table[(CHIPS - place[0]) % CHIPS, place[1]]
-        send(out.at[table[place]], land.at[back], s_sem, r_sem.at[back // 4], at_z(*place)).start()
+        q_out[SLOT[place]] = jnp.concatenate([rows8, jnp.zeros((8, HD), F32)], axis=0).astype(BF16)
+    q_land[place_here] = q_out[SELF]
+
+    pl.semaphore_wait(barrier, len(partners))
+    for place in FAR_FIRST:
+        apart = rem(div(ups[place[0]], 4) + cube, 2)
+        send(q_out.at[SLOT[place]], q_land.at[place_here], qz_s, qz_r.at[apart], at_z(*place)).start()
 
     for i in (1, 2, 3, 4):
         loads[i].wait()
@@ -139,45 +143,32 @@
 
     for place in PLACES:
         for i in range(2):
-            kv_out[KV_SLOT[place], i * TOK:(i + 1) * TOK, :] = merged(head_of(*place), i)
-    kv_all[0, KV_SLOT[0, 0]] = kv_out[KV_SLOT[0, 0]]
-
-    pl.semaphore_wait(barrier, len(partners))
-    for place in FAR_FIRST:
-        z_send(q_out, q_land, qz_s, qz_r, Q_SLOT, place)
+            kv_out[SLOT[place], i * TOK:(i + 1) * TOK, :] = merged(head_of(*place), i)
+    kv_all[0, SELF] = kv_out[SELF]
+
     for place in NEAR_FIRST:
-        z_send(kv_out, kv_all.at[0], kz_s, kz_r, KV_SLOT, place)
+        back = SLOT[(CHIPS - place[0]) % CHIPS, place[1]]
+        send(kv_out.at[SLOT[place]], kv_all.at[0, back], kz_s, kz_r.at[back // 4], at_z(*place)).start()
 
     loads[5].start()
     send(w_hbm, w_all.at[1], w_s, w_r, at_z(0, 1)).start()
 
-    def pass_queries(t):
-        half = (zl, 1 - zl, 0, 1)[t]
-        first = t * 4 + (t * 4 == Q_SLOT[0, 0])
-        arrived(q_land.at[first:t * 4 + 4], qz_r.at[t])
-        packed = q_land[t * 4:(t + 1) * 4].astype(F32)[:, 0:8, :].reshape(32, HD)
-        part = slice(t // 2 * 32, t // 2 * 32 + 32)
-        q_all[half, 7, part, :] = packed.astype(BF16)
+    for half, remote, sem in ((cube, 7, 0), (1 - cube, 8, 1)):
+        arrived(q_land.at[0:remote], qz_r.at[sem])
+        packed = q_land[pl.ds(half * 8, 8)].astype(F32)[:, 0:8, :].reshape(64, HD)
+        q_row[7, half] = packed.astype(BF16)
         for p in range(7):
-            send(
-                q_all.at[half, 7, part], q_all.at[half, p, part], qy_s, qy_r.at[p // 4], at_y(ORDER[p])
-            ).start()
+            send(q_row.at[7, half], q_row.at[p, half], qy_s, qy_r.at[p // 4], at_y(ORDER[p])).start()
 
     def pass_entries(g):
-        first = g * 4 + (g * 4 == KV_SLOT[0, 0])
+        first = g * 4 + (g * 4 == SELF)
         arrived(kv_all.at[0, first:g * 4 + 4], kz_r.at[g])
         part = slice(g * 4, g * 4 + 4)
         for s in (2, 1, 3):
             send(kv_all.at[0, part], kv_all.at[s, part], kx_s, kx_r.at[g], at_x(s)).start()
 
-    pass_queries(3)
-    pass_entries(0)
-    pass_queries(0)
-    pass_queries(1)
-    pass_entries(1)
-    pass_entries(2)
-    pass_queries(2)
-    pass_entries(3)
+    for g in range(4):
+        pass_entries(g)
 
     group = NX * 4 * TOK
     for g in range(4):
@@ -190,8 +181,19 @@
     def own(p, g):
         return p == 7 and g == 2
 
+    def rows_for(k):
+        there = (1 - zl if k < 2 else zl) * 2 + cores[k % 2]
+        return pl.ds(pl.multiple_of(there * 16, 16), 16)
+
     for near in (1, 0):
-        arrived(q_all.at[:, near * 4:near * 4 + 4 - near], qy_r.at[near])
+        arrived(q_row.at[near * 4:near * 4 + 4 - near], qy_r.at[near])
+        for p in range(near * 4, near * 4 + 4):
+            rows = q_row[p].astype(F32).reshape(2, 4, 2, 8, HD)
+            for i in range(2):
+                halves = [
+                    jnp.where(mine == i, rows[c, k, 0], rows[c, k, 1]) for k in range(4) for c in range(2)
+                ]
+                q_all[i, p] = jnp.concatenate(halves, axis=0).astype(BF16)
     for unit in range(4):
         keys = jnp.concatenate(
             [kv_all[:, g * 4:g * 4 + 4, 0:TOK, :].reshape(group, HD) for g in range(4)], axis=0
@@ -217,7 +219,7 @@
             for k in range(4):
                 if not own(p, k):
                     dev = at_o(NY - ORDER[p], k < 2, k % 2)
-                    piece = o_out.at[i, p, k * 16:(k + 1) * 16]
+                    piece = o_out.at[i, p, rows_for(k)]
                     send(piece, o_in.at[i, k, p], o_s.at[i, k], o_r.at[i, k], dev).start()
 
     row8 = lax.broadcasted_iota(jnp.int32, (8, HD), 0)
@@ -225,18 +227,17 @@
     row = lax.broadcasted_iota(jnp.int32, (16, HD), 0)
     lane = lax.broadcasted_iota(jnp.int32, (16, HD), 1)
     straight = rem(lane, 16) == row
-    swapped = rem(lane, 16) == rem(row + 8, 16)
     valid = lax.broadcasted_iota(jnp.int32, (8, CW), 0) < count
     for i in range(2):
         st_in[i, 2, 7] = st_out[i, 3]
-        o_in[i, 2, 7] = o_out[i, 7, 32:48]
+        o_in[i, 2, 7] = o_out[i, 7, rows_for(2)]
         levels = []
         for k in range(4):
             arrived(st_in.at[i, k, 0:8 - (k == 2)], t_r.at[i, k])
             seen = jnp.concatenate([st_in[i, k, p] for p in range(NY)], axis=0)
             seen = pltpu.roll(seen, 0, 1, stride=16, stride_axis=0)
-            low, high = (pltpu.roll(seen, (HD + shift - k * 16) % HD, 1) for shift in (0, 64))
-            moved = jnp.where(rem(row8, 2) == 0, low, high)
+            low = pltpu.roll(seen, rem(HD - quarter * 16, HD), 1)
+            moved = jnp.where(rem(row8, 2) == 0, low, pltpu.roll(low, 64, 1))
             levels.append(jnp.sum(jnp.where(div(lane8, 16) == row8, moved, 0.0), axis=0, keepdims=True))
         levels = jnp.concatenate(levels + levels, axis=0)
         peak = levels
@@ -252,8 +253,6 @@
         for k in range(4):
             arrived(o_in.at[i, k, 0:8 - (k == 2)], o_r.at[i, k])
             mix = jnp.where(straight, shares[k:k + 1, :], 0.0)
-            if k < 2 and i == 0:
-                mix = jnp.where(zl == 1, mix, jnp.where(swapped, shares[k:k + 1, :], 0.0))
             mean.append(jnp.dot(mix.astype(BF16), o_in[i, k].reshape(HD, HD), preferred_element_type=F32))
         heads4 = [jnp.where(zl == z, mean[2 + dc], mean[dc]) for dc in range(2) for z in range(2)]
         rows = jnp.concatenate(heads4, axis=1).astype(BF16)
@@ -267,32 +266,32 @@
                 w = jnp.concatenate([w_all[0, :, start:start + CW], w_all[1, :, start:start + CW]], axis=0)
                 sides.append(jnp.dot(rows, w, preferred_element_type=F32))
             for n in range(2):
-                b = n * 2 + i
                 block = jnp.concatenate([side[n * 8:(n + 1) * 8] for side in sides], axis=0)
-                p_out[b, ci] = block.astype(BF16)
-                if b:
-                    send(p_out.at[b, ci], p_in.at[b, ci], p_s.at[b], p_r.at[b], at_p(b)).start()
-
-    for b in (2, 1, 3):
-        arrived(p_in.at[b], p_r.at[b])
+                p_out[i, n, ci] = block.astype(BF16)
+            for slot, n in ((0, 1 - cube),) if i == 0 else ((1, cube), (2, 1 - cube)):
+                dev = at_p(n, mine if i == 0 else 1 - mine)
+                send(p_out.at[i, n, ci], p_in.at[slot, ci], p_s.at[slot], p_r.at[slot], dev).start()
+
+    for slot in range(3):
+        arrived(p_in.at[slot], p_r.at[slot])
     for ci in range(CHUNKS):
-        total = p_out[0, ci].astype(F32)
-        for b in (1, 3, 2):
-            total = total + p_in[b, ci].astype(F32)
+        total = p_out[0, cube, ci].astype(F32)
+        for n in range(3):
+            total = total + p_in[n, ci].astype(F32)
         out_ref[:, ci * CW:(ci + 1) * CW] = jnp.where(valid, total[0:8], 0.0)
         out_ref[:, HALF + ci * CW:HALF + (ci + 1) * CW] = jnp.where(valid, total[8:16], 0.0)
 
     left(q_out.at[0:15], qz_s)
     left(kv_out.at[0:15], kz_s)
     send(w_hbm, w_all.at[1], w_s, w_r, at_z(0, 1)).wait_send()
-    left(q_all.at[:, 0:7], qy_s)
+    left(q_row.at[0:7], qy_s)
     left(kv_all.at[1:4], kx_s)
     for i in range(2):
         for k in range(4):
             left(st_in.at[i, k, 0:8 - (k == 2)], t_s.at[i, k])
             left(o_in.at[i, k, 0:8 - (k == 2)], o_s.at[i, k])
-    for b in range(1, NZ):
-        left(p_out.at[b], p_s.at[b])
+    for slot in range(3):
+        left(p_out.at[0, 0], p_s.at[slot])
 
 
 def on_device(fresh_query, fresh_entries, cached_entries, recompute_rows, valid_counts, out_weight, out_gate):
@@ -314,6 +313,7 @@
             pltpu.VMEM((HEADS, 2 * TOK, HD), BF16),
             pltpu.VMEM((HEADS, 16, HD), BF16),
             pltpu.VMEM((NX, HEADS, 2 * TOK, HD), BF16),
+            pltpu.VMEM((NY, 2, 64, HD), BF16),
             pltpu.VMEM((2, NY, 64, HD), BF16),
             pltpu.VMEM((HD + 16, 4 * HEADS * TOK), BF16),
             pltpu.VMEM((2, NY, 64, HD), BF16),
@@ -321,15 +321,15 @@
             pltpu.VMEM((2, 4, 1, HD), F32),
             pltpu.VMEM((2, 4, NY, 1, HD), F32),
             pltpu.VMEM((2, 2 * HD, D), BF16),
-            pltpu.VMEM((NZ, CHUNKS, 16, CW), BF16),
-            pltpu.VMEM((NZ, CHUNKS, 16, CW), BF16),
+            pltpu.VMEM((2, 2, CHUNKS, 16, CW), BF16),
+            pltpu.VMEM((3, CHUNKS, 16, CW), BF16),
             dma((6,)),
-            dma, dma((4,)), dma, dma((4,)),
+            dma, dma((2,)), dma, dma((4,)),
             dma, dma,
             dma, dma((2,)),
             dma, dma((4,)),
             dma((2, 4)), dma((2, 4)), dma((2, 4)), dma((2, 4)),
-            dma((NZ,)), dma((NZ,)),
+            dma((3,)), dma((3,)),
         ],
         compiler_params=pltpu.CompilerParams(
             collective_id=0, has_side_effects=True, vmem_limit_bytes=60 * 1024 * 1024

time: 46.2 us -> 46 us (level)
  no operation moved by 1% of the time
where the time goes in v7:
time: 46 us; the launch traced here: 45.8 us
  Pallas kernels  44.5 us (97%)
  between operations  0.68 us (1%)
  other arithmetic  0.63 us (1%)
    pallas_call x1, Pallas kernels, on_device(): pl.pallas_call(kernel, out_shape=pltpu.VMEM((8, D), F32), in_specs=[pl.Bl...  44.5 us

profile of v7, /device:TPU:1, one launch (start us, length us, event | category | flops | bytes accessed | tf_op | source)
XLA Modules:
  0.0 45.8 jit_solution(5633660046204056944)
XLA Ops:
  0.0 0.0 copy-start
  0.7 44.5 %shard_map.73 = f32[8,3072]{1,0:T(8,128)S(1)} custom-call(bf16[7,2048]{1,0:T(8,128)(2,1)} %q_hbm.1, bf16[7,2,2048]{2,1,0:T(2,128)(2,1)} %bitcast.3, bf16[2,16,2048]{2,1,0:T(8,128)(2,1)} %cached_hbm.1, s32[1,7]{1,0:T(1,128)} %rows_hbm.1, s32[1,1]{1,0:T(1,128)} %bitcast.2.cnt_hbm, bf16[256,3072]{1,0:T(8,128)(2,1)} %w_hbm.1), custom_call_target="tpu_custom_call" | custom-call | tf_op jit(solution)/shard_map/pallas_call | solution.py:300
  45.1 0.0 copy-done
  45.1 0.6 %multiply_convert_fusion = bf16[7,3072]{1,0:T(8,128)(2,1)} fusion(f32[8,3072]{1,0:T(8,128)S(1)} %shard_map.73, f32[3072]{0:T(1024)S(1)} %copy-done), kind=kLoop, calls=%fused_computation | loop fusion | flops 43008 | bytes 141312 | tf_op jit(solution)/shard_map/convert_element_type | solution.py:338
Async XLA Ops:
  0.0 45.1 %copy-start = (f32[3072]{0:T(1024)S(1)}, f32[3072]{0:T(1024)}, u32[]{:S(2)}) copy-start(f32[3072]{0:T(1024)} %param.13) | copy-start | bytes 36868

commit v8 on v7

--- a/solution.py
+++ b/solution.py
@@ -97,12 +97,13 @@
         pltpu.make_async_copy(cnt_hbm, cnt_in, sem_in.at[4]),
         pltpu.make_async_copy(w_hbm, w_all.at[0], sem_in.at[5]),
     ]
+    loads[0].start()
     barrier = pltpu.get_barrier_semaphore()
     partners = [at_z(dz, dc) for dz, dc in FAR_FIRST]
     partners += [at_y(dy) for dy in ORDER[:7]] + [at_x(dx) for dx in (2, 1, 3)]
     for dev in partners[:15]:
         pl.semaphore_signal(barrier, inc=1, device_id=dev, device_id_type=MESH)
-    for load in loads[:5]:
+    for load in loads[1:5]:
         load.start()
     for dev in partners[15:]:
         pl.semaphore_signal(barrier, inc=1, device_id=dev, device_id_type=MESH)
@@ -215,8 +216,8 @@
                 if not own(p, k):
                     dev = at_o(NY - ORDER[p], k < 2, k % 2)
                     send(st_out.at[i, p // 2], st_in.at[i, k, p], t_s.at[i, k], t_r.at[i, k], dev).start()
-        for p in range(base, base + 4):
-            for k in range(4):
+        for k in range(4):
+            for p in range(base, base + 4):
                 if not own(p, k):
                     dev = at_o(NY - ORDER[p], k < 2, k % 2)
                     piece = o_out.at[i, p, rows_for(k)]

time: 46 us -> 46 us (level)
  no operation moved by 1% of the time
where the time goes in v8:
time: 46 us; the launch traced here: 45.8 us
  Pallas kernels  44.5 us (97%)
  between operations  0.68 us (1%)
  other arithmetic  0.63 us (1%)
    pallas_call x1, Pallas kernels, on_device(): pl.pallas_call(kernel, out_shape=pltpu.VMEM((8, D), F32), in_specs=[pl.Bl...  44.5 us

profile of v8, /device:TPU:1, one launch (start us, length us, event | category | flops | bytes accessed | tf_op | source)
XLA Modules:
  0.0 45.8 jit_solution(16265985018537231104)
XLA Ops:
  0.0 0.0 copy-start
  0.7 44.5 %shard_map.73 = f32[8,3072]{1,0:T(8,128)S(1)} custom-call(bf16[7,2048]{1,0:T(8,128)(2,1)} %q_hbm.1, bf16[7,2,2048]{2,1,0:T(2,128)(2,1)} %bitcast.3, bf16[2,16,2048]{2,1,0:T(8,128)(2,1)} %cached_hbm.1, s32[1,7]{1,0:T(1,128)} %rows_hbm.1, s32[1,1]{1,0:T(1,128)} %bitcast.2.cnt_hbm, bf16[256,3072]{1,0:T(8,128)(2,1)} %w_hbm.1), custom_call_target="tpu_custom_call" | custom-call | tf_op jit(solution)/shard_map/pallas_call | solution.py:301
  45.2 0.0 copy-done
  45.2 0.6 %multiply_convert_fusion = bf16[7,3072]{1,0:T(8,128)(2,1)} fusion(f32[8,3072]{1,0:T(8,128)S(1)} %shard_map.73, f32[3072]{0:T(1024)S(1)} %copy-done), kind=kLoop, calls=%fused_computation | loop fusion | flops 43008 | bytes 141312 | tf_op jit(solution)/shard_map/convert_element_type | solution.py:339
Async XLA Ops:
  0.0 45.2 %copy-start = (f32[3072]{0:T(1024)S(1)}, f32[3072]{0:T(1024)}, u32[]{:S(2)}) copy-start(f32[3072]{0:T(1024)} %param.13) | copy-start | bytes 36868
